TPU v7x, 512 devices: a whole 4x8x8 slice. The times are simulated.
512 devices in a mesh: dom: 32 (over z, y_hi), blk: 16 (over y_lo, x, core).
Axes of the slice: x: 4, y: 8 (y_hi: 4, y_lo: 2; y = y_hi * 2 + y_lo), z: 8, core: 2. Of those that a mesh axis runs over, the one named last changes fastest.
Arguments:
- queries: bfloat16 [65536, 512], P(('dom', 'blk')), may hold values from -22 to 22
- keys: bfloat16 [65536, 512], P(('dom', 'blk')), may hold values from -22 to 22
- values: bfloat16 [65536, 512], P(('dom', 'blk')), may hold values from -12 to 12
- grad_out: bfloat16 [65536, 512], P(('dom', 'blk')), may hold values from -6 to 6
- tile_keys: int32 [512, 16], P(('dom', 'blk')), may hold values from 0 to 15, as said below
- tile_count: int32 [512], P(('dom', 'blk')), may hold values from 1 to 16, as said below
- send_rows: int32 [512, 32, 16], P(('dom', 'blk')), may hold values from 0 to 127, as said below
Outputs:
- attended: bfloat16 [65536, 512], P(('dom', 'blk'))
- grad_q: bfloat16 [65536, 512], P(('dom', 'blk'))
- grad_k: bfloat16 [65536, 512], P(('dom', 'blk'))
- grad_v: bfloat16 [65536, 512], P(('dom', 'blk'))
Inputs may be any that keep to these rules, and one draw needn't show every extreme that they name: `tile_keys`: each row is an ordering of the 16 places of a group, and its first entry is the block's own place. `tile_count`: some block's count is 16. `send_rows`: the 16 entries for one block and one group are distinct; entries for the block's own group are not used.
All inputs are finite; a program needn't handle non-finite values.
Results may differ from a plain program's by a relative error of at most 0.027.
Values may be sent and summed in bfloat16 or wider, within the bound.
A program may use at most 64 MiB of HBM per device.

v0:
```python
import math

import jax
import jax.numpy as jnp
from jax import lax
from jax.sharding import PartitionSpec as P

HEADS = 8


def split_heads(matrix):
    return matrix.reshape(matrix.shape[0], HEADS, matrix.shape[1] // HEADS)


def head_scores(query_heads, block, width, scale):
    key_heads = split_heads(block[:, :width])
    return (
        jnp.einsum("qhe,khe->hqk", query_heads, key_heads, preferred_element_type=jnp.float32)
        * scale
    )


def tile_terms(query_heads, cotangent, log_total, delta, block, scores, width, scale):
    key_heads = split_heads(block[:, :width])
    value_heads = split_heads(block[:, width:])
    chances = jnp.exp(scores - log_total[:, :, None])
    weights = chances.astype(jnp.bfloat16)
    moves = jnp.einsum("qhe,khe->hqk", cotangent, value_heads, preferred_element_type=jnp.float32)
    slopes = (chances * (moves - delta[:, :, None])).astype(jnp.bfloat16)
    query_part = jnp.einsum("hqk,khe->qhe", slopes, key_heads, preferred_element_type=jnp.float32)
    key_part = (
        jnp.einsum("hqk,qhe->khe", slopes, query_heads, preferred_element_type=jnp.float32) * scale
    )
    value_part = jnp.einsum("hqk,qhe->khe", weights, cotangent, preferred_element_type=jnp.float32)
    row_count = block.shape[0]
    terms = jnp.concatenate(
        [key_part.reshape(row_count, width), value_part.reshape(row_count, width)], axis=1
    )
    return (query_part, terms.astype(jnp.bfloat16))


def on_device(queries, keys, values, grad_out, tile_keys, tile_count, send_rows):
    block_rows, width = queries.shape
    slot_rows = send_rows.shape[2]
    group_size = lax.axis_size("blk")
    domain_size = lax.axis_size("dom")
    scale = 1.0 / math.sqrt(width // HEADS)
    paired = jnp.concatenate([keys, values], axis=1)
    query_heads = split_heads(queries)
    cotangent = split_heads(grad_out)
    outgoing = paired[send_rows[0]]
    incoming = lax.all_to_all(outgoing, "dom", split_axis=0, concat_axis=0, tiled=True)
    distant = incoming.reshape(domain_size * slot_rows, 2 * width)
    alive = jnp.repeat(jnp.arange(domain_size) != lax.axis_index("dom"), slot_rows)
    distant_scores = jnp.where(
        alive[None, None, :], head_scores(query_heads, distant, width, scale), -jnp.inf
    )
    gathered = lax.all_gather(paired, "blk", axis=0, tiled=True)
    order = tile_keys[0]
    listed = tile_count[0]

    def fetch(slot_index):
        return lax.dynamic_slice_in_dim(gathered, order[slot_index] * block_rows, block_rows, 0)

    def first_pass(slot_index, carry):
        peak, total = carry
        scores = head_scores(query_heads, fetch(slot_index), width, scale)
        higher = jnp.maximum(peak, jnp.max(scores, axis=2))
        total = total * jnp.exp(peak - higher) + jnp.sum(
            jnp.exp(scores - higher[:, :, None]), axis=2
        )
        return (higher, total)

    start_peak = jnp.max(distant_scores, axis=2)
    start_total = jnp.sum(jnp.exp(distant_scores - start_peak[:, :, None]), axis=2)
    peak, total = lax.fori_loop(0, listed, first_pass, (start_peak, start_total))
    log_total = peak + jnp.log(total)

    def attend(block, scores):
        weights = jnp.exp(scores - log_total[:, :, None]).astype(jnp.bfloat16)
        return jnp.einsum(
            "hqk,khe->qhe",
            weights,
            split_heads(block[:, width:]),
            preferred_element_type=jnp.float32,
        )

    def second_pass(slot_index, summed):
        block = fetch(slot_index)
        return summed + attend(block, head_scores(query_heads, block, width, scale))

    summed = lax.fori_loop(0, listed, second_pass, attend(distant, distant_scores))
    attended = summed.reshape(block_rows, width).astype(jnp.bfloat16)
    delta = jnp.einsum(
        "qhe,qhe->hq", cotangent, split_heads(attended), preferred_element_type=jnp.float32
    )
    query_grad, distant_terms = tile_terms(
        query_heads, cotangent, log_total, delta, distant, distant_scores, width, scale
    )
    returned = lax.all_to_all(
        distant_terms.reshape(domain_size, slot_rows, 2 * width),
        "dom",
        split_axis=0,
        concat_axis=0,
        tiled=True,
    )
    picks = (send_rows[0].reshape(-1)[:, None] == jnp.arange(block_rows)[None, :]).astype(
        jnp.bfloat16
    )
    home = jnp.einsum(
        "sr,sc->rc", picks, returned.reshape(-1, 2 * width), preferred_element_type=jnp.float32
    )

    def query_step(slot_index, carry):
        grad_sum, table = carry
        block = fetch(slot_index)
        scores = head_scores(query_heads, block, width, scale)
        part, terms = tile_terms(
            query_heads, cotangent, log_total, delta, block, scores, width, scale
        )
        table = lax.dynamic_update_slice_in_dim(
            table, terms.astype(jnp.float32), order[slot_index] * block_rows, 0
        )
        return (grad_sum + part, table)

    table = jnp.zeros((group_size * block_rows, 2 * width), jnp.float32)
    query_grad, table = lax.fori_loop(0, listed, query_step, (query_grad, table))
    near = lax.psum_scatter(
        table.astype(jnp.bfloat16), "blk", scatter_dimension=0, tiled=True
    ).astype(jnp.float32)
    combined = near + home
    grad_q = (query_grad * scale).reshape(block_rows, width).astype(jnp.bfloat16)
    grad_k = combined[:, :width].astype(jnp.bfloat16)
    grad_v = combined[:, width:].astype(jnp.bfloat16)
    return (attended, grad_q, grad_k, grad_v)


def solution(mesh):
    in_specs = (
        P(("dom", "blk"), None),
        P(("dom", "blk"), None),
        P(("dom", "blk"), None),
        P(("dom", "blk"), None),
        P(("dom", "blk"), None),
        P(("dom", "blk")),
        P(("dom", "blk"), None, None),
    )
    out_specs = (
        P(("dom", "blk"), None),
        P(("dom", "blk"), None),
        P(("dom", "blk"), None),
        P(("dom", "blk"), None),
    )
    return jax.shard_map(
        on_device, mesh=mesh, in_specs=in_specs, out_specs=out_specs, check_vma=False
    )
```

profile of v0, /device:TPU:1, one launch (start us, length us, event | category | flops | bytes accessed | tf_op | source)
XLA Modules:
  0.0 363.2 jit_solution(5436953296254952471)
XLA Ops:
  10.7 4.4 %gather_fusion = bf16[512,1024]{1,0:T(8,128)(2,1)} fusion(bf16[128,1024]{1,0:T(8,128)(2,1)} %copy-done, s32[1024]{0:T(1024)S(1)} %pad_clamp_fusion), kind=kCustom, calls=%fused_computation | custom fusion | bytes 2099200 | tf_op jit(solution)/shard_map/gather | solution.py:51
  15.1 16.6 %all-to-all-start = ((bf16[32,16,1024]{2,1,0:T(8,128)(2,1)}), bf16[32,16,1024]{2,1,0:T(8,128)(2,1)S(1)}, u32[]{:S(2)}, u32[]{:S(2)}) async-start(bf16[32,16,1024]{2,1,0:T(8,128)(2,1)} %bitcast.18), calls=%async_computation | async-start | bytes 2097152 | tf_op jit(solution)/shard_map/all_to_all | solution.py:52
  32.5 38.7 %all-to-all-done = bf16[32,16,1024]{2,1,0:T(8,128)(2,1)S(1)} async-done(((bf16[32,16,1024]{2,1,0:T(8,128)(2,1)}), bf16[32,16,1024]{2,1,0:T(8,128)(2,1)S(1)}, u32[]{:S(2)}, u32[]{:S(2)}) %all-to-all-start) | async-done | bytes 1048608 | tf_op jit(solution)/shard_map/all_to_all | solution.py:52
  71.5 1.0 copy.26
  73.5 3.9 %all-gather.2.cloned.1.call-done = bf16[2048,1024]{1,0:T(8,128)(2,1)} async-done(((bf16[128,1024]{1,0:T(8,128)(2,1)}), bf16[2048,1024]{1,0:T(8,128)(2,1)}) %all-gather.2.cloned.1.call-update) | async-done | bytes 4194320 | tf_op jit(solution)/shard_map/all_gather | solution.py:58
  77.4 6.5 %copy.29 = bf16[2048,1024]{0,1:T(8,128)(2,1)} copy(bf16[2048,1024]{1,0:T(8,128)(2,1)} %all-gather.2.cloned.1.call-done) | data formatting | bytes 8388608 | tf_op jit(solution)/shard_map/while | solution.py:76
  83.9 17.0 %while.34 = (s32[]{:T(128)}, f32[8,128]{1,0:T(8,128)S(1)}, f32[8,128]{1,0:T(8,128)S(1)}, s32[]{:T(128)}, s32[16]{0:T(128)S(1)}, /*index=5*/bf16[2048,1024]{0,1:T...) while((s32[]{:T(128)}, f32[8,128]{1,0:T(8,128)S(1)}, ...), condition=%wide.region_5.6_spmd, body=%wide.region_2.5_spmd.sunk | while | flops 17303560 | bytes 1626333 | solution.py:76
  101.4 17.7 %while.35 = (s32[]{:T(128)}, f32[128,8,64]{0,2,1:T(8,128)S(1)}, s32[]{:T(128)}, s32[16]{0:T(128)S(1)}, bf16[2048,1024]{0,1:T(8,128)(2,1)}, /*index=5*/bf16[128,8...) while((s32[]{:T(128)}, f32[128,8,64]{0,2,1:T(8,128)S(1)}, ...), condition=%wide.region_7.8_spmd, body=%wide.region_6.7_spmd.sunk | while | flops 34013192 | bytes 1446133 | solution.py:92
  103.4 1.0 constant_dynamic-slice_fusion.6
  106.8 1.0 constant_dynamic-slice_fusion.6
  110.2 1.0 constant_dynamic-slice_fusion.6
  113.6 1.0 constant_dynamic-slice_fusion.6
  117.0 1.0 constant_dynamic-slice_fusion.6
  119.2 1.8 fusion.19
  121.0 1.1 copy-done.1
  122.4 2.5 broadcast_in_dim.34.clone
  124.9 26.7 %while.36 = (s32[]{:T(128)}, f32[128,8,64]{0,2,1:T(8,128)S(1)}, bf16[2048,1024]{1,0:T(8,128)(2,1)}, s32[]{:T(128)}, s32[16]{0:T(128)S(1)}, /*index=5*/bf16[2048,...) while((s32[]{:T(128)}, f32[128,8,64]{0,2,1:T(8,128)S(1)}, ...), condition=%wide.region_9.10_spmd, body=%wide.region_8.9_spmd.sunk | while | flops 85458952 | bytes 6168849 | solution.py:127
  126.8 1.0 fusion.99
  132.0 1.0 fusion.99
  137.2 1.0 fusion.99
  142.4 1.0 fusion.99
  147.6 1.0 fusion.99
  151.6 1.7 fusion.25
  153.3 1.7 copy.39
  155.0 1.9 concatenate.17
  156.9 1.3 fusion.26
  158.2 1.8 copy.41
  160.6 1.1 pad_maximum_fusion
  161.7 89.4 %all-to-all-start.1 = ((bf16[32,16,1024]{2,1,0:T(8,128)(2,1)}), bf16[32,16,1024]{2,1,0:T(8,128)(2,1)S(1)}, u32[]{:S(2)}, u32[]{:S(2)}) async-start(bf16[32,16,1024]{2,1,0:T(8,128)(2,1)} %pad_maximum_fusion), calls=%async_computation.2 | async-start | bytes 2097152 | tf_op jit(solution)/shard_map/all_to_all | solution.py:100
  252.9 14.6 %all-to-all-done.1 = bf16[32,16,1024]{2,1,0:T(8,128)(2,1)S(1)} async-done(((bf16[32,16,1024]{2,1,0:T(8,128)(2,1)}), bf16[32,16,1024]{2,1,0:T(8,128)(2,1)S(1)}, u32[]{:S(2)}, u32[]{:S(2)}) %all-to-all-start.1) | async-done | bytes 1048608 | tf_op jit(solution)/shard_map/all_to_all | solution.py:100
  267.5 86.7 %reduce-scatter.2.cloned.1.call-done = bf16[128,1024]{1,0:T(8,128)(2,1)} async-done(((bf16[2048,1024]{1,0:T(8,128)(2,1)}), bf16[128,1024]{1,0:T(8,128)(2,1)}) %reduce-scatter.2.cloned.1.call-update) | async-done | bytes 262160 | tf_op jit(solution)/shard_map/reduce_scatter | solution.py:128
  354.2 1.4 fusion.27
  (138 shorter events, 38.4 us)
Async XLA Ops:
  7.2 70.2 %all-gather.2.cloned.1.call-start = ((), (), s32[]{:S(2)}) async-start(), calls=%async_computation.3 | async-start | bytes 4456448 | tf_op jit(solution)/shard_map/all_gather | solution.py:58
  9.0 0.7 copy-start
  15.1 16.9 %copy-start.5 = (bf16[128,512]{1,0:T(8,128)(2,1)S(1)}, bf16[128,512]{1,0:T(8,128)(2,1)}, u32[]{:S(2)}) copy-start(bf16[128,512]{1,0:T(8,128)(2,1)} %param.16) | copy-start | bytes 393220
  15.1 17.0 %copy-start.6 = (bf16[128,512]{1,0:T(8,128)(2,1)S(1)}, bf16[128,512]{1,0:T(8,128)(2,1)}, u32[]{:S(2)}) copy-start(bf16[128,512]{1,0:T(8,128)(2,1)} %param.13) | copy-start | bytes 393220
  15.1 56.1 %all-to-all-start = ((bf16[32,16,1024]{2,1,0:T(8,128)(2,1)}), bf16[32,16,1024]{2,1,0:T(8,128)(2,1)S(1)}, u32[]{:S(2)}, u32[]{:S(2)}) async-start(bf16[32,16,1024]{2,1,0:T(8,128)(2,1)} %bitcast.18), calls=%async_computation | async-start | bytes 2097152 | tf_op jit(solution)/shard_map/all_to_all | solution.py:52
  31.8 322.4 %reduce-scatter.2.cloned.1.call-start = ((), (), s32[]{:S(2)}) async-start(), calls=%async_computation.4 | async-start | bytes 4456448 | tf_op jit(solution)/shard_map/reduce_scatter | solution.py:128
  71.5 2.0 copy-start.2
  73.5 10.4 %copy-start.8 = (s32[1,16]{1,0:T(1,128)S(1)}, s32[1,16]{1,0:T(1,128)}, u32[]{:S(2)}) copy-start(s32[1,16]{1,0:T(1,128)} %param.17) | copy-start | bytes 196
  83.9 17.0 %copy-start.4 = (bf16[512,512]{0,1:T(8,128)(2,1)S(1)}, bf16[512,512]{0,1:T(8,128)(2,1)}, u32[]{:S(2)}) copy-start(bf16[512,512]{0,1:T(8,128)(2,1)} %copy.26) | copy-start | bytes 1572868
  119.2 2.9 copy-start.3
  121.0 1.1 copy-start.1
  160.6 90.6 %copy-start.7 = (s32[1,32,16]{1,2,0:T(8,128)S(1)}, s32[1,32,16]{1,2,0:T(8,128)}, u32[]{:S(2)}) copy-start(s32[1,32,16]{1,2,0:T(8,128)} %param.19) | copy-start | bytes 6148
  161.7 105.8 %all-to-all-start.1 = ((bf16[32,16,1024]{2,1,0:T(8,128)(2,1)}), bf16[32,16,1024]{2,1,0:T(8,128)(2,1)S(1)}, u32[]{:S(2)}, u32[]{:S(2)}) async-start(bf16[32,16,1024]{2,1,0:T(8,128)(2,1)} %pad_maximum_fusion), calls=%async_computation.2 | async-start | bytes 2097152 | tf_op jit(solution)/shard_map/all_to_all | solution.py:100
Sparse Core Ops, SparseCore 0:
  10.1 67.2 all-gather.1
  151.7 202.4 reduce-scatter.1
where the time goes:
time: 368 us; the launch traced here: 363 us
  waiting for transfers between devices  144 us (39%)
  starting transfers between devices  106 us (29%)
  local copies, waits for them, and re-layouts  55.4 us (15%)
  loops' own time  22.3 us (6%)
  matrix products  18.3 us (5%)
  between operations  14.3 us (4%)
    all_to_all x1, starting transfers between devices, on_device(): lax.all_to_all(distant_terms.reshape(domain_size, slot_rows, 2 * width),...  89.4 us
    reduce_scatter x1, waiting for transfers between devices, on_device(): lax.psum_scatter(table.astype(jnp.bfloat16), 'blk', scatter_dimension=0,...  86.7 us
    all_to_all x1, waiting for transfers between devices, on_device(): lax.all_to_all(outgoing, 'dom', split_axis=0, concat_axis=0, tiled=True)  38.7 us
    all_to_all x1, starting transfers between devices, on_device(): lax.all_to_all(outgoing, 'dom', split_axis=0, concat_axis=0, tiled=True)  16.6 us
    all_to_all x1, waiting for transfers between devices, on_device(): lax.all_to_all(distant_terms.reshape(domain_size, slot_rows, 2 * width),...  14.6 us
    slice x12, local copies, waits for them, and re-layouts, head_scores(): key_heads = split_heads(block[:, :width])  9.86 us
    dynamic_slice x15, local copies, waits for them, and re-layouts, fetch(): order[slot_index] * block_rows  8.8 us
    another operation x1, loops' own time, on_device(): lax.fori_loop(0, listed, first_pass, (start_peak, start_total))  7.5 us
  transfers between devices with their start and end apart: 4, of which 4 were waited for; matrix products, arithmetic and copies ran while one was open for 6% of the time, Pallas kernels for 0%

commit v1 on v0

v1 whole, which is shorter than its diff:
```python
import functools

import jax
import jax.numpy as jnp
from jax import lax
from jax.experimental import pallas as pl
from jax.experimental.pallas import tpu as pltpu
from jax.sharding import PartitionSpec as P

HEADS = 8
PAIRS = 4
PHASES = 2
PER_PHASE = PAIRS // PHASES
BLOCK = 128
SLOT = 16
HIDDEN = -1e30
MESH = pl.DeviceIdType.MESH
F32 = jnp.float32
BF16 = jnp.bfloat16


def dot_nn(a, b):
    return lax.dot_general(a, b, (((1,), (0,)), ((), ())), preferred_element_type=F32)


def dot_nt(a, b):
    return lax.dot_general(a, b, (((1,), (1,)), ((), ())), preferred_element_type=F32)


def dot_tn(a, b):
    return lax.dot_general(a, b, (((0,), (0,)), ((), ())), preferred_element_type=F32)


def lanes_of(pair):
    return pl.ds(pl.multiple_of(pair * 128, 128), 128)


def kernel(
    n_dom, n_blk,
    q_ref, k_ref, v_ref, g_ref, order_ref, count_ref, rows_ref,
    att_ref, dq_ref, dk_ref, dv_ref,
    kv, qg, far_out, far_in, terms, ret, stats_out, stats_in,
    qst, gst, kst, vst, picks, bias, far_bias,
    s_near, p_near, peak, m_near, l_near, a_near, factor, delta_ref, far_dq, near_dk, near_dv, stat_cols,
    ag_send, ag_recv, far_send, far_recv, ret_send, ret_recv, stat_send, stat_recv,
):
    me_d = lax.axis_index("dom")
    me_b = lax.axis_index("blk")
    far_rows = n_dom * SLOT
    near_rows = n_blk * BLOCK
    chips = n_blk // 2

    barrier = pltpu.get_barrier_semaphore()

    def greet_dom(step, carry):
        pl.semaphore_signal(barrier, inc=1, device_id=(lax.rem(me_d + step, n_dom), me_b), device_id_type=MESH)
        return carry

    def greet_blk(step, carry):
        pl.semaphore_signal(barrier, inc=1, device_id=(me_d, lax.rem(me_b + step, n_blk)), device_id_type=MESH)
        return carry

    lax.fori_loop(1, n_blk, greet_blk, 0)
    lax.fori_loop(1, n_dom, greet_dom, 0)

    kv[me_b, 0] = k_ref[...]
    kv[me_b, 1] = v_ref[...]
    qg[me_b, 0] = q_ref[...]
    qg[me_b, 1] = g_ref[...]
    node = lax.broadcasted_iota(jnp.int32, (BLOCK, far_rows), 0)
    picks[...] = jnp.where(rows_ref[...] == node, 1.0, 0.0).astype(BF16)
    low = lax.broadcasted_iota(jnp.int32, (BLOCK, 128), 1) < 64

    def prepare(pair, carry):
        lanes = lanes_of(pair)
        phase = pair // PER_PHASE
        place = lax.rem(pair, PER_PHASE) * 256
        k_lanes = pl.ds(pl.multiple_of(place, 128), 128)
        v_lanes = pl.ds(pl.multiple_of(place + 128, 128), 128)
        k_own, v_own = k_ref[:, lanes], v_ref[:, lanes]
        spread = picks[...]
        far_out[phase, :, :, k_lanes] = dot_tn(spread, k_own).astype(BF16).reshape(n_dom, SLOT, 128)
        far_out[phase, :, :, v_lanes] = dot_tn(spread, v_own).astype(BF16).reshape(n_dom, SLOT, 128)
        for target, rows, scale in (
            (qst, q_ref[:, lanes], 0.125),
            (gst, g_ref[:, lanes], 1.0),
            (kst, k_own, 0.125),
            (vst, v_own, 1.0),
        ):
            wide = rows.astype(F32) * scale
            target[pair, 0:BLOCK, :] = jnp.where(low, wide, 0.0).astype(BF16)
            target[pair, BLOCK : 2 * BLOCK, :] = jnp.where(low, 0.0, wide).astype(BF16)
        return carry

    lax.fori_loop(0, PAIRS, prepare, 0)

    blank = jnp.zeros((SLOT, PER_PHASE * 256), BF16)
    for phase in range(PHASES):
        far_in[phase, me_d] = blank
        ret[phase, me_d] = blank
    tile = lax.broadcasted_iota(jnp.int32, (1, near_rows), 1) // BLOCK
    hidden = jnp.full((1, near_rows), HIDDEN, F32)
    for t in range(n_blk):
        wanted = jnp.where(t < count_ref[0], order_ref[0, t], -1)
        hidden = jnp.where(tile == wanted, 0.0, hidden)
    bias[...] = hidden
    slot_group = lax.broadcasted_iota(jnp.int32, (1, far_rows), 1) // SLOT
    far_bias[...] = jnp.where(slot_group == me_d, HIDDEN, 0.0)
    peak[...] = jnp.full(peak.shape, -3e38, F32)

    pl.semaphore_wait(barrier, n_dom + n_blk - 2)

    core = lax.rem(me_b, 2)
    x0 = lax.rem(me_b // 2, 4)
    y0 = me_b // 8
    x_right, x_left, x_far = lax.rem(x0 + 1, 4), lax.rem(x0 + 3, 4), lax.rem(x0 + 2, 4)
    y1, other = 1 - y0, 1 - core

    def block_id(y, x, c):
        return (y * 4 + x) * 2 + c

    sibling = block_id(y0, x0, other)
    right, left = block_id(y0, x_right, core), block_id(y0, x_left, core)
    across = block_id(y1, x0, core)
    started = []

    def send(part, block, device, half=None):
        buffer = (kv, qg)[part]
        ref = buffer.at[block] if half is None else buffer.at[block, half]
        copy = pltpu.make_async_remote_copy(
            src_ref=ref,
            dst_ref=ref,
            send_sem=ag_send.at[len(started)],
            recv_sem=ag_recv.at[part, block, 0 if half is None else half],
            device_id=(me_d, device),
            device_id_type=MESH,
        )
        copy.start()
        started.append(copy)

    def arrived(part, block, half=None):
        buffer = (kv, qg)[part]
        ref = buffer.at[block] if half is None else buffer.at[block, half]
        sem = ag_recv.at[part, block, 0 if half is None else half]
        pltpu.make_async_copy(ref, ref, sem).wait()

    def gather_own(part):
        for device in (right, left, across, sibling):
            send(part, me_b, device)

    def gather_ring(part, y):
        from_left, from_right = block_id(y, x_left, core), block_id(y, x_right, core)
        arrived(part, from_left)
        send(part, from_left, right, 0)
        send(part, from_left, sibling)
        arrived(part, from_right)
        send(part, from_right, left, 1)
        send(part, from_right, sibling)

    def gather_across(part):
        block = block_id(y1, x0, core)
        arrived(part, block)
        for device in (right, left, sibling):
            send(part, block, device)

    def gather_far(part, y):
        block = block_id(y, x_far, core)
        arrived(part, block, 0)
        arrived(part, block, 1)
        send(part, block, sibling)

    gather_own(0)

    def spread_order(step):
        hops_z, hops_y = step // 4, lax.rem(step, 4)
        dz = jnp.where(lax.rem(hops_z, 2) == 1, (hops_z + 1) // 2, 8 - hops_z // 2)
        dy = jnp.where(lax.rem(hops_y, 2) == 1, (hops_y + 1) // 2, 4 - hops_y // 2)
        z, y = lax.rem(me_d // 4 + dz, 8), lax.rem(lax.rem(me_d, 4) + dy, 4)
        return z * 4 + y

    def exchange(source, target, send_sem, recv_sem, phase):
        def one(step, carry):
            group = spread_order(step)
            pltpu.make_async_remote_copy(
                src_ref=source.at[phase, group],
                dst_ref=target.at[phase, me_d],
                send_sem=send_sem.at[phase],
                recv_sem=recv_sem.at[phase],
                device_id=(group, me_b),
                device_id_type=MESH,
            ).start()
            return carry

        lax.fori_loop(1, n_dom, one, 0)

    def exchanged(buffer, sem, phase):
        ref = buffer.at[phase, pl.ds(0, n_dom - 1)]
        pltpu.make_async_copy(ref, ref, sem.at[phase]).wait()

    for phase in range(PHASES):
        exchange(far_out, far_in, far_send, far_recv, phase)

    def score_chip(y, x):
        chip = y * 4 + x

        def one(pair, carry):
            key_rows = kv[pl.ds(2 * chip, 2), 0, :, lanes_of(pair)].reshape(256, 128)
            row = bias[:, pl.ds(pl.multiple_of(chip * 256, 256), 256)]
            scores = dot_nt(qst[pair], key_rows) + row
            s_near[chip, pair] = scores
            peak[pair] = jnp.maximum(peak[pair], jnp.maximum(scores[:, :128], scores[:, 128:]))
            return carry

        lax.fori_loop(0, PAIRS, one, 0)

    def score_sibling(y, x):
        arrived(0, block_id(y, x, other))
        score_chip(y, x)

    score_sibling(y0, x0)
    gather_ring(0, y0)
    gather_across(0)
    score_sibling(y0, x_left)
    score_sibling(y0, x_right)
    gather_far(0, y0)
    score_sibling(y1, x0)
    gather_ring(0, y1)
    score_sibling(y0, x_far)
    gather_far(0, y1)
    gather_own(1)
    score_sibling(y1, x_left)
    score_sibling(y1, x_right)
    score_sibling(y1, x_far)

    def weigh(pair, carry):
        top = jnp.max(peak[pair], axis=1, keepdims=True)

        def one(chip, held):
            total, out = held
            exps = jnp.exp(s_near[chip, pair] - top)
            total = total + exps[:, :128] + exps[:, 128:]
            narrow = exps.astype(BF16)
            p_near[chip, pair] = narrow
            value_rows = kv[pl.ds(2 * chip, 2), 1, :, lanes_of(pair)].reshape(256, 128)
            return total, out + dot_nn(narrow, value_rows)

        zero = jnp.zeros((256, 128), F32)
        total, out = lax.fori_loop(0, chips, one, (zero, zero))
        m_near[pair] = top
        l_near[pair] = jnp.sum(total, axis=1, keepdims=True)
        a_near[pair] = out
        return carry

    gather_ring(1, y0)
    lax.fori_loop(0, PAIRS // 2, weigh, 0)
    gather_across(1)
    gather_far(1, y0)
    lax.fori_loop(PAIRS // 2, PAIRS, weigh, 0)
    gather_ring(1, y1)

    column = lax.broadcasted_iota(jnp.int32, (BLOCK, 128), 1)

    def far_pair(phase, place):
        pair = phase * PER_PHASE + place
        lanes = lanes_of(pair)
        k_lanes, v_lanes = pl.ds(place * 256, 128), pl.ds(place * 256 + 128, 128)
        key_rows = far_in[phase, :, :, k_lanes].reshape(far_rows, 128)
        value_rows = far_in[phase, :, :, v_lanes].reshape(far_rows, 128)
        queries, cotangent = qst[pair], gst[pair]
        scores = dot_nt(queries, key_rows) + far_bias[...]
        moves = dot_nt(cotangent, value_rows)
        top = jnp.max(scores, axis=1, keepdims=True)
        exps = jnp.exp(scores - top)
        total = jnp.sum(exps, axis=1, keepdims=True)
        far_att = dot_nn(exps.astype(BF16), value_rows)
        near_top = m_near[pair]
        highest = jnp.maximum(top, near_top)
        near_scale, far_scale = jnp.exp(near_top - highest), jnp.exp(top - highest)
        whole = near_scale * l_near[pair] + far_scale * total
        near_scale, far_scale = near_scale / whole, far_scale / whole
        out = a_near[pair] * near_scale + far_att * far_scale
        attended = jnp.where(low, out[:BLOCK], out[BLOCK:]).astype(BF16)
        att_ref[:, lanes] = attended
        product = g_ref[:, lanes].astype(F32) * attended.astype(F32)
        delta0 = jnp.sum(jnp.where(low, product, 0.0), axis=1, keepdims=True)
        delta1 = jnp.sum(jnp.where(low, 0.0, product), axis=1, keepdims=True)
        delta = jnp.concatenate([delta0, delta1], axis=0)
        log_total = highest + jnp.log(whole)
        chances = exps * far_scale
        weights = chances.astype(BF16)
        slopes = (chances * (moves - delta)).astype(BF16)
        terms[phase, :, :, k_lanes] = dot_tn(slopes, queries).astype(BF16).reshape(n_dom, SLOT, 128)
        terms[phase, :, :, v_lanes] = dot_tn(weights, cotangent).astype(BF16).reshape(n_dom, SLOT, 128)
        far_dq[pair] = dot_nn(slopes, key_rows)
        factor[pair] = near_scale
        delta_ref[pair] = delta
        held = stat_cols[...]
        held = jnp.where(column == 2 * pair, log_total[:BLOCK], held)
        held = jnp.where(column == 2 * pair + 1, log_total[BLOCK:], held)
        held = jnp.where(column == HEADS + 2 * pair, delta0, held)
        held = jnp.where(column == HEADS + 2 * pair + 1, delta1, held)
        stat_cols[...] = held

    stat_cols[...] = jnp.zeros((BLOCK, 128), F32)
    for phase in range(PHASES):
        exchanged(far_in, far_recv, phase)
        for place in range(PER_PHASE):
            far_pair(phase, place)
        exchange(terms, ret, ret_send, ret_recv, phase)
        if phase == 0:
            gather_far(1, y1)

    stat_rows = stat_cols[...].T
    for block in range(n_blk):
        row = bias[:, block * BLOCK : (block + 1) * BLOCK]
        stats_out[block, 0:HEADS, :] = stat_rows[0:HEADS] - row
        stats_out[block, HEADS : 2 * HEADS, :] = stat_rows[HEADS : 2 * HEADS]
    stats_in[me_b] = stats_out[me_b]

    def tell(step, carry):
        block = lax.rem(me_b + step, n_blk)
        pltpu.make_async_remote_copy(
            src_ref=stats_out.at[block],
            dst_ref=stats_in.at[me_b],
            send_sem=stat_send.at[0],
            recv_sem=stat_recv.at[0],
            device_id=(me_d, block),
            device_id_type=MESH,
        ).start()
        return carry

    lax.fori_loop(1, n_blk, tell, 0)

    def query_pair(pair, carry):
        lanes = lanes_of(pair)
        cotangent, delta = gst[pair], delta_ref[pair]

        def one(chip, held):
            key_rows = kv[pl.ds(2 * chip, 2), 0, :, lanes].reshape(256, 128)
            value_rows = kv[pl.ds(2 * chip, 2), 1, :, lanes].reshape(256, 128)
            moves = dot_nt(cotangent, value_rows)
            slopes = (p_near[chip, pair].astype(F32) * (moves - delta)).astype(BF16)
            return held + dot_nn(slopes, key_rows)

        near = lax.fori_loop(0, chips, one, jnp.zeros((256, 128), F32))
        both = (far_dq[pair] + near * factor[pair]) * 0.125
        dq_ref[:, lanes] = jnp.where(low, both[:BLOCK], both[BLOCK:]).astype(BF16)
        return carry

    lax.fori_loop(0, PAIRS, query_pair, 0)

    all_stats = stats_in.at[pl.ds(0, n_blk - 1)]
    pltpu.make_async_copy(all_stats, all_stats, stat_recv.at[0]).wait()
    for y in (y0, y1):
        for x in (x0, x_left, x_right, x_far):
            arrived(1, block_id(y, x, other))

    def key_pair(pair, carry):
        lanes = lanes_of(pair)
        own_keys, own_values = kst[pair], vst[pair]

        def stat_row(chip, first):
            parts = [
                jnp.concatenate([stats_in[2 * chip, pl.ds(row, 1), :], stats_in[2 * chip + 1, pl.ds(row, 1), :]], axis=1)
                for row in (first, first + 1)
            ]
            return parts

        def one(chip, held):
            sum_k, sum_v = held
            query_rows = qg[pl.ds(2 * chip, 2), 0, :, lanes].reshape(256, 128)
            grad_rows = qg[pl.ds(2 * chip, 2), 1, :, lanes].reshape(256, 128)
            scores = dot_nt(own_keys, query_rows)
            moves = dot_nt(own_values, grad_rows)
            log0, log1 = stat_row(chip, 2 * pair)
            delta0, delta1 = stat_row(chip, HEADS + 2 * pair)
            chances0 = jnp.exp(scores[:BLOCK] - log0)
            chances1 = jnp.exp(scores[BLOCK:] - log1)
            slopes0 = chances0 * (moves[:BLOCK] - delta0)
            slopes1 = chances1 * (moves[BLOCK:] - delta1)
            weights = jnp.concatenate([chances0, chances1], axis=0).astype(BF16)
            slopes = jnp.concatenate([slopes0, slopes1], axis=0).astype(BF16)
            return sum_k + dot_nn(slopes, query_rows), sum_v + dot_nn(weights, grad_rows)

        zero = jnp.zeros((256, 128), F32)
        sum_k, sum_v = lax.fori_loop(0, chips, one, (zero, zero))
        near_dk[pair] = jnp.where(low, sum_k[:BLOCK], sum_k[BLOCK:]) * 0.125
        near_dv[pair] = jnp.where(low, sum_v[:BLOCK], sum_v[BLOCK:])
        return carry

    lax.fori_loop(0, PAIRS, key_pair, 0)

    for phase in range(PHASES):
        exchanged(ret, ret_recv, phase)
        for place in range(PER_PHASE):
            pair = phase * PER_PHASE + place
            cols = slice(pair * 128, pair * 128 + 128)
            spread = picks[...]
            back_k = ret[phase, :, :, place * 256 : place * 256 + 128].reshape(far_rows, 128)
            back_v = ret[phase, :, :, place * 256 + 128 : place * 256 + 256].reshape(far_rows, 128)
            dk_ref[:, cols] = (near_dk[pair] + dot_nn(spread, back_k)).astype(BF16)
            dv_ref[:, cols] = (near_dv[pair] + dot_nn(spread, back_v)).astype(BF16)

    for copy in started:
        copy.wait_send()
    for phase in range(PHASES):
        exchanged(far_out, far_send, phase)
        exchanged(terms, ret_send, phase)
    sent_stats = stats_out.at[pl.ds(0, n_blk - 1)]
    pltpu.make_async_copy(sent_stats, sent_stats, stat_send.at[0]).wait()


def on_device(n_dom, n_blk, queries, keys, values, grad_out, tile_keys, tile_count, send_rows):
    rows, width = queries.shape
    far_rows = n_dom * SLOT
    chips = n_blk // 2
    vmem = pl.BlockSpec(memory_space=pltpu.VMEM)
    smem = pl.BlockSpec(memory_space=pltpu.SMEM)
    far_shape = (PHASES, n_dom, SLOT, PER_PHASE * 256)
    stack = pltpu.VMEM((PAIRS, 256, 128), BF16)
    wide = pltpu.VMEM((PAIRS, 256, 128), F32)
    thin = pltpu.VMEM((PAIRS, 256, 1), F32)
    own = pltpu.VMEM((PAIRS, BLOCK, 128), F32)
    dma = pltpu.SemaphoreType.DMA
    return pl.pallas_call(
        functools.partial(kernel, n_dom, n_blk),
        out_shape=[jax.ShapeDtypeStruct((rows, width), BF16)] * 4,
        in_specs=[vmem, vmem, vmem, vmem, smem, smem, vmem],
        out_specs=[vmem] * 4,
        scratch_shapes=[
            pltpu.VMEM((n_blk, 2, BLOCK, width), BF16),
            pltpu.VMEM((n_blk, 2, BLOCK, width), BF16),
            pltpu.VMEM(far_shape, BF16),
            pltpu.VMEM(far_shape, BF16),
            pltpu.VMEM(far_shape, BF16),
            pltpu.VMEM(far_shape, BF16),
            pltpu.VMEM((n_blk, 2 * HEADS, BLOCK), F32),
            pltpu.VMEM((n_blk, 2 * HEADS, BLOCK), F32),
            stack, stack, stack, stack,
            pltpu.VMEM((BLOCK, far_rows), BF16),
            pltpu.VMEM((1, n_blk * BLOCK), F32),
            pltpu.VMEM((1, far_rows), F32),
            pltpu.VMEM((chips, PAIRS, 256, 256), F32),
            pltpu.VMEM((chips, PAIRS, 256, 256), BF16),
            wide,
            thin, thin,
            wide,
            thin, thin,
            wide,
            own, own,
            pltpu.VMEM((BLOCK, 128), F32),
            dma((34,)), dma((2, n_blk, 2)),
            dma((PHASES,)), dma((PHASES,)), dma((PHASES,)), dma((PHASES,)),
            dma((1,)), dma((1,)),
        ],
        compiler_params=pltpu.CompilerParams(
            collective_id=0, has_side_effects=True, vmem_limit_bytes=50 * 1024 * 1024
        ),
        cost_estimate=pl.CostEstimate(flops=2_500_000_000, bytes_accessed=2_000_000, transcendentals=5_000_000),
    )(queries, keys, values, grad_out, tile_keys, tile_count, send_rows.reshape(1, far_rows))


def solution(mesh):
    n_dom, n_blk = mesh.shape["dom"], mesh.shape["blk"]
    both = ("dom", "blk")
    flat = P(both, None)
    return jax.shard_map(
        functools.partial(on_device, n_dom, n_blk),
        mesh=mesh,
        in_specs=(flat, flat, flat, flat, flat, P(both), P(both, None, None)),
        out_specs=(flat,) * 4,
        check_vma=False,
    )
```

time: 368 us -> 111 us (0.30); the launches traced: 363 us -> 111 us
  waiting for transfers between devices: 144 us -> 0 us
  starting transfers between devices: 106 us -> 0 us
  Pallas kernels: 0 us -> 102 us
  local copies, waits for them, and re-layouts: 55.4 us -> 7.66 us
  loops' own time: 22.3 us -> 0 us
  matrix products: 18.3 us -> 0 us
  between operations: 14.3 us -> 1.29 us
    all_to_all x2 -> x0, starting transfers between devices: 106 us -> none  [the longest x1 89.4 us: on_device(): lax.all_to_all(distant_terms.reshape(domain_size, slot_rows, 2 * width),...]
    pallas_call x0 -> x1, Pallas kernels: none -> 102 us  [on_device(): pl.pallas_call(functools.partial(kernel, n_dom, n_blk), out_shape=[jax.Sh...]
    reduce_scatter x1 -> x0, waiting for transfers between devices: 86.7 us -> none  [on_device(): lax.psum_scatter(table.astype(jnp.bfloat16), 'blk', scatter_dimension=0,...]
    all_to_all x2 -> x0, waiting for transfers between devices: 53.3 us -> none  [the longest x1 38.7 us: on_device(): lax.all_to_all(outgoing, 'dom', split_axis=0, concat_axis=0, tiled=True)]
    another operation x3 -> x0, loops' own time: 22.3 us -> none  [the longest x1 7.5 us: on_device(): lax.fori_loop(0, listed, first_pass, (start_peak, start_total))]
    dot_general x42 -> x0, matrix products: 18.3 us -> none  [the longest x11 3.55 us: head_scores(): jnp.einsum('qhe,khe->hqk', query_heads, key_heads, preferred_element_type...]
    slice x19 -> x0, local copies, waits for them, and re-layouts: 16.6 us -> none  [the longest x12 9.86 us: head_scores(): key_heads = split_heads(block[:, :width])]
    dynamic_slice x15 -> x0, local copies, waits for them, and re-layouts: 8.8 us -> none  [fetch(): order[slot_index] * block_rows]
  transfers between devices with their start and end apart: 4 -> 0, of which waited for: 4 -> 0; matrix products, arithmetic and copies ran while one was open for 6% -> 0% of each run, Pallas kernels for 0% -> 0%
where the time goes in v1:
time: 111 us
  Pallas kernels  102 us (92%)
  local copies, waits for them, and re-layouts  7.66 us (7%)
  between operations  1.29 us (1%)
    pallas_call x1, Pallas kernels, on_device(): pl.pallas_call(functools.partial(kernel, n_dom, n_blk), out_shape=[jax.Sh...  102 us
    unnamed x15, local copies, waits for them, and re-layouts  7.58 us

profile of v1, /device:TPU:1, one launch (start us, length us, event | category | flops | bytes accessed | tf_op | source)
XLA Modules:
  0.0 110.7 jit_solution(2929197927474595672)
XLA Ops:
  1.3 0.8 copy.12
  2.0 0.0 copy-start.4
  2.1 0.1 reshape.11.rows_ref
  2.1 0.6 copy-done.4
  2.7 0.0 copy-start
  2.7 0.9 copy-done
  3.6 0.0 copy-start.1
  3.6 0.9 copy-done.1
  4.5 0.0 copy-start.2
  4.5 0.9 copy-done.2
  5.4 0.0 copy-start.3
  5.4 0.9 copy-done.3
  6.3 101.7 %shard_map.102 = (bf16[128,512]{1,0:T(8,128)(2,1)S(1)}, bf16[128,512]{1,0:T(8,128)(2,1)S(1)}, bf16[128,512]{1,0:T(8,128)(2,1)S(1)}, bf16[128,512]{1,0:T(8,128)(2,1)S(1)}) custom-call(bf16[128,512]{1,0:T(8,128)(2,1)S(1)} %copy-done, bf16[128,512]{1,0:T(8,128)(2,1)S(1)} %copy-done.1, bf16[128,512]{1,0:T(8,128)(2,1)S(1)} %copy-done.2, ...), custom_call_target="tpu_custom_call" | custom-call | flops 2500000000 | bytes 2000000 | tf_op jit(solution)/shard_map/pallas_call | solution.py:425
  108.1 0.7 copy.18
  108.7 0.7 copy.19
  109.4 0.7 copy.20
  110.0 0.7 copy.21
Async XLA Ops:
  2.0 0.7 copy-start.4
  2.7 0.9 copy-start
  3.6 0.9 copy-start.1
  4.5 0.9 copy-start.2
  5.4 0.9 copy-start.3

commit v2 on v1

v2 whole, which is shorter than its diff:
```python
import functools

import jax
import jax.numpy as jnp
from jax import lax
from jax.experimental import pallas as pl
from jax.experimental.pallas import tpu as pltpu
from jax.sharding import PartitionSpec as P

HEADS = 8
PAIRS = 4
PHASES = 2
PER_PHASE = PAIRS // PHASES
BLOCK = 128
SLOT = 16
RELAYED = 11
HIDDEN = -1e30
MESH = pl.DeviceIdType.MESH
F32 = jnp.float32
BF16 = jnp.bfloat16


def dot_nn(a, b):
    return lax.dot_general(a, b, (((1,), (0,)), ((), ())), preferred_element_type=F32)


def dot_nt(a, b):
    return lax.dot_general(a, b, (((1,), (1,)), ((), ())), preferred_element_type=F32)


def dot_tn(a, b):
    return lax.dot_general(a, b, (((0,), (0,)), ((), ())), preferred_element_type=F32)


def lanes_of(pair):
    return pl.ds(pl.multiple_of(pair * 128, 128), 128)


def kernel(
    n_dom, n_blk,
    q_in, k_in, v_in, g_in, order_in, count_ref, rows_in,
    att_out, dq_out, dk_out, dv_out,
    kv, qg, far_out, far_in, terms, ret, out_relay, back_relay, stats_out, stats_in,
    order_ref, rows_ref, qst, gst, kst, vst, picks, bias, far_bias,
    s_near, p_near, peak, m_near, l_near, a_near, factor, delta_ref, far_dq, near_dk, near_dv, stat_cols,
    in_sem, ag_send, ag_recv, far_send, far_recv, far_mid, far_next, ret_send, ret_recv, ret_mid, ret_next,
    stat_send, stat_recv, att_ref, dq_ref, dk_ref, dv_ref, out_sem,
):
    me_d = lax.axis_index("dom")
    me_b = lax.axis_index("blk")
    far_rows = n_dom * SLOT
    near_rows = n_blk * BLOCK
    row_blocks = n_blk // 2
    row_keys = row_blocks * BLOCK

    barrier = pltpu.get_barrier_semaphore()

    def greet_dom(step, carry):
        pl.semaphore_signal(barrier, inc=1, device_id=(lax.rem(me_d + step, n_dom), me_b), device_id_type=MESH)
        return carry

    def greet_blk(step, carry):
        pl.semaphore_signal(barrier, inc=1, device_id=(me_d, lax.rem(me_b + step, n_blk)), device_id_type=MESH)
        return carry

    lax.fori_loop(1, n_blk, greet_blk, 0)
    lax.fori_loop(1, n_dom, greet_dom, 0)

    loads = [
        pltpu.make_async_copy(source, target, in_sem.at[number])
        for number, (source, target) in enumerate(
            (
                (order_in, order_ref),
                (rows_in, rows_ref),
                (k_in, kv.at[me_b, 0]),
                (v_in, kv.at[me_b, 1]),
                (q_in, qg.at[me_b, 0]),
                (g_in, qg.at[me_b, 1]),
            )
        )
    ]
    for load in loads:
        load.start()
    for load in loads:
        load.wait()
    k_ref, v_ref, q_ref, g_ref = kv.at[me_b, 0], kv.at[me_b, 1], qg.at[me_b, 0], qg.at[me_b, 1]
    group_of = lax.broadcasted_iota(jnp.int32, (n_dom, far_rows), 1) // SLOT
    widen = jnp.where(group_of == lax.broadcasted_iota(jnp.int32, (n_dom, far_rows), 0), 1.0, 0.0).astype(BF16)
    repeated = dot_nn(rows_ref[0].astype(F32).astype(BF16), widen)
    slot_of = lax.rem(lax.broadcasted_iota(jnp.int32, (SLOT, far_rows), 1), SLOT)
    slot = lax.broadcasted_iota(jnp.int32, (SLOT, far_rows), 0)
    row_list = jnp.sum(jnp.where(slot_of == slot, repeated, 0.0), axis=0, keepdims=True)
    node = lax.broadcasted_iota(jnp.int32, (BLOCK, far_rows), 0).astype(F32)
    hits = jnp.where(row_list == node, 1.0, 0.0)
    picks[...] = hits.astype(BF16)
    spread = hits.T.astype(BF16)
    low = lax.broadcasted_iota(jnp.int32, (BLOCK, 128), 1) < 64

    for pair in range(PAIRS):
        lanes = slice(pair * 128, pair * 128 + 128)
        phase, place = divmod(pair, PER_PHASE)
        k_own, v_own = k_ref[:, lanes], v_ref[:, lanes]
        for own, first in ((k_own, place * 256), (v_own, place * 256 + 128)):
            moved = dot_nn(spread, own).astype(BF16).reshape(n_dom, SLOT, 128)
            far_out[phase, :, :, first : first + 128] = moved
        for target, rows, scale in (
            (qst, q_ref[:, lanes], 0.125),
            (gst, g_ref[:, lanes], 1.0),
            (kst, k_own, 0.125),
            (vst, v_own, 1.0),
        ):
            wide = rows.astype(F32) * scale
            target[pair, 0:BLOCK, :] = jnp.where(low, wide, 0.0).astype(BF16)
            target[pair, BLOCK : 2 * BLOCK, :] = jnp.where(low, 0.0, wide).astype(BF16)

    blank = jnp.zeros((SLOT, PER_PHASE * 256), BF16)
    for phase in range(PHASES):
        far_in[phase, me_d] = blank
        ret[phase, me_d] = blank
    tile = lax.broadcasted_iota(jnp.int32, (1, near_rows), 1) // BLOCK
    hidden = jnp.full((1, near_rows), HIDDEN, F32)
    for t in range(n_blk):
        wanted = jnp.where(t < count_ref[0], order_ref[0, t], -1)
        hidden = jnp.where(tile == wanted, 0.0, hidden)
    bias[...] = hidden
    slot_group = lax.broadcasted_iota(jnp.int32, (1, far_rows), 1) // SLOT
    far_bias[...] = jnp.where(slot_group == me_d, HIDDEN, 0.0)
    peak[...] = jnp.full(peak.shape, -3e38, F32)

    pl.semaphore_wait(barrier, n_dom + n_blk - 2)

    core = lax.rem(me_b, 2)
    x0 = lax.rem(me_b // 2, 4)
    y0 = me_b // 8
    x_right, x_left, x_far = lax.rem(x0 + 1, 4), lax.rem(x0 + 3, 4), lax.rem(x0 + 2, 4)
    y1, other = 1 - y0, 1 - core

    def block_id(y, x, c):
        return (y * 4 + x) * 2 + c

    sibling = block_id(y0, x0, other)
    right, left = block_id(y0, x_right, core), block_id(y0, x_left, core)
    across = block_id(y1, x0, core)
    started = []

    def send(part, block, device, half=None):
        buffer = (kv, qg)[part]
        ref = buffer.at[block] if half is None else buffer.at[block, half]
        copy = pltpu.make_async_remote_copy(
            src_ref=ref,
            dst_ref=ref,
            send_sem=ag_send.at[len(started)],
            recv_sem=ag_recv.at[part, block, 0 if half is None else half],
            device_id=(me_d, device),
            device_id_type=MESH,
        )
        copy.start()
        started.append(copy)

    def arrived(part, block, half=None):
        buffer = (kv, qg)[part]
        ref = buffer.at[block] if half is None else buffer.at[block, half]
        sem = ag_recv.at[part, block, 0 if half is None else half]
        pltpu.make_async_copy(ref, ref, sem).wait()

    def gather_own(part):
        for device in (right, left, across, sibling):
            send(part, me_b, device)

    def gather_ring(part, y):
        from_left, from_right = block_id(y, x_left, core), block_id(y, x_right, core)
        arrived(part, from_left)
        send(part, from_left, right, 0)
        send(part, from_left, sibling)
        arrived(part, from_right)
        send(part, from_right, left, 1)
        send(part, from_right, sibling)

    def gather_across(part):
        block = block_id(y1, x0, core)
        arrived(part, block)
        for device in (right, left, sibling):
            send(part, block, device)

    def gather_far(part, y):
        block = block_id(y, x_far, core)
        arrived(part, block, 0)
        arrived(part, block, 1)
        send(part, block, sibling)

    gather_own(0)

    def zigzag(step, size):
        return jnp.where(lax.rem(step, 2) == 1, (step + 1) // 2, lax.rem(size - step // 2, size))

    def at_offset(dz, dy):
        z = lax.rem(me_d // 4 + dz + 16, 8)
        y = lax.rem(lax.rem(me_d, 4) + dy + 8, 4)
        return z * 4 + y

    def legs(step, way):
        along_z = step < 4
        dz = jnp.where(along_z, 4, zigzag(step - 4, 8))
        dy = jnp.where(along_z, step, 2)
        first_z = jnp.where(along_z, 2 * way, dz)
        first_y = jnp.where(dy == 2, way, dy)
        return dz, dy, first_z, first_y

    def push(source, target, send_sem, recv_sem, group):
        pltpu.make_async_remote_copy(
            src_ref=source,
            dst_ref=target,
            send_sem=send_sem,
            recv_sem=recv_sem,
            device_id=(group, me_b),
            device_id_type=MESH,
        ).start()

    def exchange(source, relay, target, send_sem, mid_sem, recv_sem, phase):
        way = 1 - 2 * phase

        def indirect(step, carry):
            dz, dy, first_z, first_y = legs(step, way)
            push(
                source.at[phase, at_offset(dz, dy)], relay.at[phase, step],
                send_sem.at[phase], mid_sem.at[phase], at_offset(first_z, first_y),
            )
            return carry

        def direct(step, carry):
            group = at_offset(zigzag(step // 3, 8), zigzag(lax.rem(step, 3), 4))
            push(source.at[phase, group], target.at[phase, me_d], send_sem.at[phase], recv_sem.at[phase], group)
            return carry

        lax.fori_loop(0, RELAYED, indirect, 0)
        lax.fori_loop(1, 21, direct, 0)

    def pass_on(relay, target, mid_sem, next_sem, recv_sem, phase):
        way = 1 - 2 * phase
        pltpu.make_async_copy(relay.at[phase], relay.at[phase], mid_sem.at[phase]).wait()

        def one(step, carry):
            dz, dy, first_z, first_y = legs(step, way)
            push(
                relay.at[phase, step], target.at[phase, at_offset(-first_z, -first_y)],
                next_sem.at[phase], recv_sem.at[phase], at_offset(dz - first_z, dy - first_y),
            )
            return carry

        lax.fori_loop(0, RELAYED, one, 0)

    def exchanged(buffer, sem, phase):
        ref = buffer.at[phase, pl.ds(0, n_dom - 1)]
        pltpu.make_async_copy(ref, ref, sem.at[phase]).wait()

    for phase in range(PHASES):
        exchange(far_out, out_relay, far_in, far_send, far_mid, far_recv, phase)

    def score_chip(row, y, x):
        chip = y * 4 + x
        hidden_keys = bias[:, pl.ds(pl.multiple_of(chip * 256, 256), 256)]
        lanes = pl.ds(pl.multiple_of(x * 256, 256), 256)
        for pair in range(PAIRS):
            key_rows = kv[pl.ds(2 * chip, 2), 0, :, pair * 128 : pair * 128 + 128].reshape(256, 128)
            scores = dot_nt(qst[pair], key_rows) + hidden_keys
            s_near[row, pair, :, lanes] = scores
            peak[row, pair] = jnp.maximum(peak[row, pair], jnp.maximum(scores[:, :128], scores[:, 128:]))

    def score_sibling(row, x):
        y = (y0, y1)[row]
        arrived(0, block_id(y, x, other))
        score_chip(row, y, x)

    def weigh(row, y):
        def one(pair, carry):
            top = jnp.max(peak[row, pair], axis=1, keepdims=True)
            exps = jnp.exp(s_near[row, pair] - top)
            narrow = exps.astype(BF16)
            p_near[row, pair] = narrow
            value_rows = kv[pl.ds(y * row_blocks, row_blocks), 1, :, lanes_of(pair)].reshape(row_keys, 128)
            m_near[row, pair] = top
            l_near[row, pair] = jnp.sum(exps, axis=1, keepdims=True)
            a_near[row, pair] = dot_nn(narrow, value_rows)
            return carry

        lax.fori_loop(0, PAIRS, one, 0)

    out_path = (out_relay, far_in, far_mid, far_next, far_recv)
    back_path = (back_relay, ret, ret_mid, ret_next, ret_recv)

    score_sibling(0, x0)
    gather_ring(0, y0)
    gather_across(0)
    score_sibling(0, x_left)
    score_sibling(0, x_right)
    gather_far(0, y0)
    pass_on(*out_path, 0)
    score_sibling(0, x_far)
    score_sibling(1, x0)
    gather_ring(0, y1)
    weigh(0, y0)
    pass_on(*out_path, 1)
    gather_far(0, y1)
    gather_own(1)
    score_sibling(1, x_left)
    score_sibling(1, x_right)
    score_sibling(1, x_far)
    weigh(1, y1)

    column = lax.broadcasted_iota(jnp.int32, (BLOCK, 128), 1)

    def far_pair(phase, place):
        pair = phase * PER_PHASE + place
        lanes = lanes_of(pair)
        k_lanes, v_lanes = pl.ds(place * 256, 128), pl.ds(place * 256 + 128, 128)
        key_rows = far_in[phase, :, :, k_lanes].reshape(far_rows, 128)
        value_rows = far_in[phase, :, :, v_lanes].reshape(far_rows, 128)
        queries, cotangent = qst[pair], gst[pair]
        scores = dot_nt(queries, key_rows) + far_bias[...]
        moves = dot_nt(cotangent, value_rows)
        top = jnp.max(scores, axis=1, keepdims=True)
        exps = jnp.exp(scores - top)
        total = jnp.sum(exps, axis=1, keepdims=True)
        far_att = dot_nn(exps.astype(BF16), value_rows)
        top0, top1 = m_near[0, pair], m_near[1, pair]
        highest = jnp.maximum(top, jnp.maximum(top0, top1))
        scale0, scale1 = jnp.exp(top0 - highest), jnp.exp(top1 - highest)
        far_scale = jnp.exp(top - highest)
        whole = scale0 * l_near[0, pair] + scale1 * l_near[1, pair] + far_scale * total
        scale0, scale1, far_scale = scale0 / whole, scale1 / whole, far_scale / whole
        out = a_near[0, pair] * scale0 + a_near[1, pair] * scale1 + far_att * far_scale
        attended = jnp.where(low, out[:BLOCK], out[BLOCK:]).astype(BF16)
        att_ref[:, lanes] = attended
        product = g_ref[:, lanes].astype(F32) * attended.astype(F32)
        delta0 = jnp.sum(jnp.where(low, product, 0.0), axis=1, keepdims=True)
        delta1 = jnp.sum(jnp.where(low, 0.0, product), axis=1, keepdims=True)
        delta = jnp.concatenate([delta0, delta1], axis=0)
        log_total = highest + jnp.log(whole)
        chances = exps * far_scale
        weights = chances.astype(BF16)
        slopes = (chances * (moves - delta)).astype(BF16)
        terms[phase, :, :, k_lanes] = dot_tn(slopes, queries).astype(BF16).reshape(n_dom, SLOT, 128)
        terms[phase, :, :, v_lanes] = dot_tn(weights, cotangent).astype(BF16).reshape(n_dom, SLOT, 128)
        far_dq[pair] = dot_nn(slopes, key_rows)
        factor[0, pair] = scale0
        factor[1, pair] = scale1
        delta_ref[pair] = delta
        held = stat_cols[...]
        held = jnp.where(column == 2 * pair, log_total[:BLOCK], held)
        held = jnp.where(column == 2 * pair + 1, log_total[BLOCK:], held)
        held = jnp.where(column == HEADS + 2 * pair, delta0, held)
        held = jnp.where(column == HEADS + 2 * pair + 1, delta1, held)
        stat_cols[...] = held

    stat_cols[...] = jnp.zeros((BLOCK, 128), F32)
    for phase in range(PHASES):
        exchanged(far_in, far_recv, phase)
        for place in range(PER_PHASE):
            far_pair(phase, place)
        exchange(terms, back_relay, ret, ret_send, ret_mid, ret_recv, phase)
        if phase == 0:
            gather_ring(1, y0)
            gather_across(1)

    stat_rows = stat_cols[...].T
    for block in range(n_blk):
        row = bias[:, block * BLOCK : (block + 1) * BLOCK]
        stats_out[block, 0:HEADS, :] = stat_rows[0:HEADS] - row
        stats_out[block, HEADS : 2 * HEADS, :] = stat_rows[HEADS : 2 * HEADS]
    stats_in[me_b] = stats_out[me_b]

    def tell(step, carry):
        block = lax.rem(me_b + step, n_blk)
        pltpu.make_async_remote_copy(
            src_ref=stats_out.at[block],
            dst_ref=stats_in.at[me_b],
            send_sem=stat_send.at[0],
            recv_sem=stat_recv.at[0],
            device_id=(me_d, block),
            device_id_type=MESH,
        ).start()
        return carry

    lax.fori_loop(1, n_blk, tell, 0)

    def query_pair(pair, carry):
        lanes = lanes_of(pair)
        cotangent, delta = gst[pair], delta_ref[pair]
        both = far_dq[pair]
        for row, y in enumerate((y0, y1)):
            blocks = pl.ds(y * row_blocks, row_blocks)
            key_rows = kv[blocks, 0, :, lanes].reshape(row_keys, 128)
            value_rows = kv[blocks, 1, :, lanes].reshape(row_keys, 128)
            moves = dot_nt(cotangent, value_rows)
            slopes = (p_near[row, pair].astype(F32) * (moves - delta)).astype(BF16)
            both += dot_nn(slopes, key_rows) * factor[row, pair]
        both *= 0.125
        dq_ref[:, lanes] = jnp.where(low, both[:BLOCK], both[BLOCK:]).astype(BF16)
        return carry

    gather_far(1, y0)
    lax.fori_loop(0, PAIRS // 2, query_pair, 0)
    pass_on(*back_path, 0)
    gather_ring(1, y1)
    lax.fori_loop(PAIRS // 2, PAIRS, query_pair, 0)
    pass_on(*back_path, 1)
    gather_far(1, y1)

    def written(number, source, target):
        return pltpu.make_async_copy(source, target, out_sem.at[number])

    att_copy, dq_copy = written(0, att_ref, att_out), written(1, dq_ref, dq_out)
    att_copy.start()
    dq_copy.start()

    all_stats = stats_in.at[pl.ds(0, n_blk - 1)]
    pltpu.make_async_copy(all_stats, all_stats, stat_recv.at[0]).wait()
    for y in (y0, y1):
        for x in (x0, x_left, x_right, x_far):
            arrived(1, block_id(y, x, other))

    def key_pair(pair, carry):
        lanes = lanes_of(pair)
        own_keys, own_values = kst[pair], vst[pair]

        def stat_row(start, row):
            return jnp.concatenate([stats_in[start + n, pl.ds(row, 1), :] for n in range(4)], axis=1)

        sum_k = sum_v = jnp.zeros((256, 128), F32)
        for start in range(0, n_blk, 4):
            query_rows = qg[start : start + 4, 0, :, lanes].reshape(4 * BLOCK, 128)
            grad_rows = qg[start : start + 4, 1, :, lanes].reshape(4 * BLOCK, 128)
            scores = dot_nt(own_keys, query_rows)
            moves = dot_nt(own_values, grad_rows)
            weights, slopes = [], []
            for head in range(2):
                rows = slice(head * BLOCK, head * BLOCK + BLOCK)
                chances = jnp.exp(scores[rows] - stat_row(start, 2 * pair + head))
                weights.append(chances.astype(BF16))
                slopes.append((chances * (moves[rows] - stat_row(start, HEADS + 2 * pair + head))).astype(BF16))
            sum_k += dot_nn(jnp.concatenate(slopes, axis=0), query_rows)
            sum_v += dot_nn(jnp.concatenate(weights, axis=0), grad_rows)
        near_dk[pair] = jnp.where(low, sum_k[:BLOCK], sum_k[BLOCK:]) * 0.125
        near_dv[pair] = jnp.where(low, sum_v[:BLOCK], sum_v[BLOCK:])
        return carry

    lax.fori_loop(0, PAIRS, key_pair, 0)

    for phase in range(PHASES):
        exchanged(ret, ret_recv, phase)
        for place in range(PER_PHASE):
            pair = phase * PER_PHASE + place
            cols = slice(pair * 128, pair * 128 + 128)
            hits = picks[...]
            back_k = ret[phase, :, :, place * 256 : place * 256 + 128].reshape(far_rows, 128)
            back_v = ret[phase, :, :, place * 256 + 128 : place * 256 + 256].reshape(far_rows, 128)
            dk_ref[:, cols] = (near_dk[pair] + dot_nn(hits, back_k)).astype(BF16)
            dv_ref[:, cols] = (near_dv[pair] + dot_nn(hits, back_v)).astype(BF16)

    dk_copy, dv_copy = written(2, dk_ref, dk_out), written(3, dv_ref, dv_out)
    dk_copy.start()
    dv_copy.start()
    for copy in started:
        copy.wait_send()
    for phase in range(PHASES):
        exchanged(far_out, far_send, phase)
        exchanged(terms, ret_send, phase)
        pltpu.make_async_copy(out_relay.at[phase], out_relay.at[phase], far_next.at[phase]).wait()
        pltpu.make_async_copy(back_relay.at[phase], back_relay.at[phase], ret_next.at[phase]).wait()
    sent_stats = stats_out.at[pl.ds(0, n_blk - 1)]
    pltpu.make_async_copy(sent_stats, sent_stats, stat_send.at[0]).wait()
    for copy in (att_copy, dq_copy, dk_copy, dv_copy):
        copy.wait()


def write_out(a, b, c, d, a_out, b_out, c_out, d_out, sems):
    pairs = ((a, a_out), (b, b_out), (c, c_out), (d, d_out))
    copies = [pltpu.make_async_copy(here, there, sems.at[n]) for n, (here, there) in enumerate(pairs)]
    for copy in copies:
        copy.start()
    for copy in copies:
        copy.wait()


def on_device(n_dom, n_blk, queries, keys, values, grad_out, tile_keys, tile_count, send_rows):
    rows, width = queries.shape
    far_rows = n_dom * SLOT
    row_keys = n_blk // 2 * BLOCK
    hbm = pl.BlockSpec(memory_space=pltpu.HBM)
    smem = pl.BlockSpec(memory_space=pltpu.SMEM)
    far_shape = (PHASES, n_dom, SLOT, PER_PHASE * 256)
    stack = pltpu.VMEM((PAIRS, 256, 128), BF16)
    relay = pltpu.VMEM((PHASES, RELAYED, SLOT, PER_PHASE * 256), BF16)
    wide = pltpu.VMEM((PAIRS, 256, 128), F32)
    wide_rows = pltpu.VMEM((2, PAIRS, 256, 128), F32)
    thin = pltpu.VMEM((PAIRS, 256, 1), F32)
    thin_rows = pltpu.VMEM((2, PAIRS, 256, 1), F32)
    whole = pltpu.VMEM((rows, width), BF16)
    own = pltpu.VMEM((PAIRS, BLOCK, 128), F32)
    dma = pltpu.SemaphoreType.DMA
    held = pl.pallas_call(
        functools.partial(kernel, n_dom, n_blk),
        out_shape=[jax.ShapeDtypeStruct((rows, width), BF16)] * 4,
        in_specs=[hbm, hbm, hbm, hbm, hbm, smem, hbm],
        out_specs=[hbm] * 4,
        scratch_shapes=[
            pltpu.VMEM((n_blk, 2, BLOCK, width), BF16),
            pltpu.VMEM((n_blk, 2, BLOCK, width), BF16),
            pltpu.VMEM(far_shape, BF16),
            pltpu.VMEM(far_shape, BF16),
            pltpu.VMEM(far_shape, BF16),
            pltpu.VMEM(far_shape, BF16),
            relay, relay,
            pltpu.VMEM((n_blk, 2 * HEADS, BLOCK), F32),
            pltpu.VMEM((n_blk, 2 * HEADS, BLOCK), F32),
            pltpu.SMEM((1, n_blk), jnp.int32),
            pltpu.VMEM((1, SLOT, n_dom), jnp.int32),
            stack, stack, stack, stack,
            pltpu.VMEM((BLOCK, far_rows), BF16),
            pltpu.VMEM((1, n_blk * BLOCK), F32),
            pltpu.VMEM((1, far_rows), F32),
            pltpu.VMEM((2, PAIRS, 256, row_keys), F32),
            pltpu.VMEM((2, PAIRS, 256, row_keys), BF16),
            wide_rows,
            thin_rows, thin_rows,
            wide_rows,
            thin_rows, thin,
            wide,
            own, own,
            pltpu.VMEM((BLOCK, 128), F32),
            dma((6,)), dma((34,)), dma((2, n_blk, 2)),
            dma((PHASES,)), dma((PHASES,)), dma((PHASES,)), dma((PHASES,)),
            dma((PHASES,)), dma((PHASES,)), dma((PHASES,)), dma((PHASES,)),
            dma((1,)), dma((1,)),
            whole, whole, whole, whole, dma((4,)),
        ],
        compiler_params=pltpu.CompilerParams(
            collective_id=0, has_side_effects=True, vmem_limit_bytes=63 * 1024 * 1024
        ),
        cost_estimate=pl.CostEstimate(flops=2_500_000_000, bytes_accessed=2_000_000, transcendentals=5_000_000),
    )(queries, keys, values, grad_out, tile_keys, tile_count, send_rows.transpose(0, 2, 1))
    return pl.pallas_call(
        write_out,
        out_shape=[jax.ShapeDtypeStruct((rows, width), BF16)] * 4,
        in_specs=[hbm] * 4,
        out_specs=[hbm] * 4,
        scratch_shapes=[dma((4,))],
        compiler_params=pltpu.CompilerParams(vmem_limit_bytes=63 * 1024 * 1024),
    )(*held)


def solution(mesh):
    n_dom, n_blk = mesh.shape["dom"], mesh.shape["blk"]
    both = ("dom", "blk")
    flat = P(both, None)
    return jax.shard_map(
        functools.partial(on_device, n_dom, n_blk),
        mesh=mesh,
        in_specs=(flat, flat, flat, flat, flat, P(both), P(both, None, None)),
        out_specs=(flat,) * 4,
        check_vma=False,
    )
```

time: 111 us -> 106 us (0.955)
  the two profiles are of different devices: /device:TPU:1 before, /device:TPU:49 now
where the time goes in v2:
time: 106 us
  Pallas kernels  105 us (99%)
  between operations  1.29 us (1%)
    pallas_call x1, Pallas kernels, on_device(): pl.pallas_call(functools.partial(kernel, n_dom, n_blk), out_shape=[jax.Sh...  87.6 us
    pallas_call x1, Pallas kernels, on_device(): pl.pallas_call(write_out, out_shape=[jax.ShapeDtypeStruct((rows, width),...  17 us

profile of v2, /device:TPU:49, one launch (start us, length us, event | category | flops | bytes accessed | tf_op | source)
XLA Modules:
  0.0 105.9 jit_solution(6957712725744815845)
XLA Ops:
  1.3 87.6 %shard_map.102 = (bf16[128,512]{1,0:T(8,128)(2,1)}, bf16[128,512]{1,0:T(8,128)(2,1)}, bf16[128,512]{1,0:T(8,128)(2,1)}, bf16[128,512]{1,0:T(8,128)(2,1)}) custom-call(bf16[128,512]{1,0:T(8,128)(2,1)} %q_in.1, bf16[128,512]{1,0:T(8,128)(2,1)} %k_in.1, bf16[128,512]{1,0:T(8,128)(2,1)} %v_in.1, bf16[128,512]{1,0:T(8,128)(2,1)} %g_in.1, s32[1,16]{1,0:T(1,128)} %order_in.1, ...), custom_call_target="tpu_custom_call" | custom-call | flops 2500000000 | bytes 2000000 | tf_op jit(solution)/shard_map/pallas_call | solution.py:501
  88.9 17.0 %shard_map.103 = (bf16[128,512]{1,0:T(8,128)(2,1)}, bf16[128,512]{1,0:T(8,128)(2,1)}, bf16[128,512]{1,0:T(8,128)(2,1)}, bf16[128,512]{1,0:T(8,128)(2,1)}) custom-call(bf16[128,512]{1,0:T(8,128)(2,1)} %get-tuple-element.8.a, bf16[128,512]{1,0:T(8,128)(2,1)} %get-tuple-element.9.b, bf16[128,512]{1,0:T(8,128)(2,1)} %get-tuple-element.10.c, ...), custom_call_target="tpu_custom_call" | custom-call | tf_op jit(solution)/shard_map/pallas_call | solution.py:542

commit v3 on v2

--- a/solution.py
+++ b/solution.py
@@ -103,16 +103,143 @@
         for own, first in ((k_own, place * 256), (v_own, place * 256 + 128)):
             moved = dot_nn(spread, own).astype(BF16).reshape(n_dom, SLOT, 128)
             far_out[phase, :, :, first : first + 128] = moved
-        for target, rows, scale in (
-            (qst, q_ref[:, lanes], 0.125),
-            (gst, g_ref[:, lanes], 1.0),
-            (kst, k_own, 0.125),
-            (vst, v_own, 1.0),
-        ):
-            wide = rows.astype(F32) * scale
+
+    pl.semaphore_wait(barrier, n_dom + n_blk - 2)
+
+    core = lax.rem(me_b, 2)
+    x0 = lax.rem(me_b // 2, 4)
+    y0 = me_b // 8
+    x_right, x_left, x_far = lax.rem(x0 + 1, 4), lax.rem(x0 + 3, 4), lax.rem(x0 + 2, 4)
+    y1, other = 1 - y0, 1 - core
+
+    def block_id(y, x, c):
+        return (y * 4 + x) * 2 + c
+
+    sibling = block_id(y0, x0, other)
+    right, left = block_id(y0, x_right, core), block_id(y0, x_left, core)
+    across = block_id(y1, x0, core)
+    started = []
+
+    def send(part, block, device, half=None):
+        buffer = (kv, qg)[part]
+        ref = buffer.at[block] if half is None else buffer.at[block, half]
+        copy = pltpu.make_async_remote_copy(
+            src_ref=ref,
+            dst_ref=ref,
+            send_sem=ag_send.at[len(started)],
+            recv_sem=ag_recv.at[part, block, 0 if half is None else half],
+            device_id=(me_d, device),
+            device_id_type=MESH,
+        )
+        copy.start()
+        started.append(copy)
+
+    def arrived(part, block, half=None):
+        buffer = (kv, qg)[part]
+        ref = buffer.at[block] if half is None else buffer.at[block, half]
+        sem = ag_recv.at[part, block, 0 if half is None else half]
+        pltpu.make_async_copy(ref, ref, sem).wait()
+
+    def gather_own(part):
+        for device in (across, right, left, sibling):
+            if part == 0 or device is not across:
+                send(part, me_b, device)
+
+    def gather_ring(part, y):
+        from_left, from_right = block_id(y, x_left, core), block_id(y, x_right, core)
+        arrived(part, from_left)
+        send(part, from_left, right, 0)
+        send(part, from_left, sibling)
+        arrived(part, from_right)
+        send(part, from_right, left, 1)
+        send(part, from_right, sibling)
+
+    def gather_across(part):
+        block = block_id(y1, x0, core)
+        arrived(part, block)
+        for device in (right, left, sibling):
+            send(part, block, device)
+
+    def gather_far(part, y):
+        block = block_id(y, x_far, core)
+        arrived(part, block, 0)
+        arrived(part, block, 1)
+        send(part, block, sibling)
+
+    gather_own(0)
+
+    def zigzag(step, size):
+        return jnp.where(lax.rem(step, 2) == 1, (step + 1) // 2, lax.rem(size - step // 2, size))
+
+    def at_offset(dz, dy):
+        z = lax.rem(me_d // 4 + dz + 16, 8)
+        y = lax.rem(lax.rem(me_d, 4) + dy + 8, 4)
+        return z * 4 + y
+
+    def legs(step, way):
+        along_z = step < 4
+        dz = jnp.where(along_z, 4, zigzag(step - 4, 8))
+        dy = jnp.where(along_z, step, 2)
+        first_z = jnp.where(along_z, 2 * way, dz)
+        first_y = jnp.where(dy == 2, way, dy)
+        return dz, dy, first_z, first_y
+
+    def push(source, target, send_sem, recv_sem, group):
+        pltpu.make_async_remote_copy(
+            src_ref=source,
+            dst_ref=target,
+            send_sem=send_sem,
+            recv_sem=recv_sem,
+            device_id=(group, me_b),
+            device_id_type=MESH,
+        ).start()
+
+    def exchange(source, relay, target, send_sem, mid_sem, recv_sem, phase):
+        way = 1 - 2 * phase
+
+        def indirect(step, carry):
+            dz, dy, first_z, first_y = legs(step, way)
+            push(
+                source.at[phase, at_offset(dz, dy)], relay.at[phase, step],
+                send_sem.at[phase], mid_sem.at[phase], at_offset(first_z, first_y),
+            )
+            return carry
+
+        def direct(step, carry):
+            group = at_offset(zigzag(step // 3, 8), zigzag(lax.rem(step, 3), 4))
+            push(source.at[phase, group], target.at[phase, me_d], send_sem.at[phase], recv_sem.at[phase], group)
+            return carry
+
+        lax.fori_loop(0, RELAYED, indirect, 0)
+        lax.fori_loop(1, 21, direct, 0)
+
+    def pass_on(relay, target, mid_sem, next_sem, recv_sem, phase):
+        way = 1 - 2 * phase
+        pltpu.make_async_copy(relay.at[phase], relay.at[phase], mid_sem.at[phase]).wait()
+
+        def one(step, carry):
+            dz, dy, first_z, first_y = legs(step, way)
+            push(
+                relay.at[phase, step], target.at[phase, at_offset(-first_z, -first_y)],
+                next_sem.at[phase], recv_sem.at[phase], at_offset(dz - first_z, dy - first_y),
+            )
+            return carry
+
+        lax.fori_loop(0, RELAYED, one, 0)
+
+    def exchanged(buffer, sem, phase):
+        ref = buffer.at[phase, pl.ds(0, n_dom - 1)]
+        pltpu.make_async_copy(ref, ref, sem.at[phase]).wait()
+
+    for phase in range(PHASES):
+        exchange(far_out, out_relay, far_in, far_send, far_mid, far_recv, phase)
+
+    for pair in range(PAIRS):
+        lanes = slice(pair * 128, pair * 128 + 128)
+        for target, source, scale in ((qst, q_ref, 0.125), (gst, g_ref, 1.0), (kst, k_ref, 0.125), (vst, v_ref, 1.0)):
+            wide = source[:, lanes].astype(F32) * scale
             target[pair, 0:BLOCK, :] = jnp.where(low, wide, 0.0).astype(BF16)
             target[pair, BLOCK : 2 * BLOCK, :] = jnp.where(low, 0.0, wide).astype(BF16)
-
     blank = jnp.zeros((SLOT, PER_PHASE * 256), BF16)
     for phase in range(PHASES):
         far_in[phase, me_d] = blank
@@ -126,135 +253,6 @@
     slot_group = lax.broadcasted_iota(jnp.int32, (1, far_rows), 1) // SLOT
     far_bias[...] = jnp.where(slot_group == me_d, HIDDEN, 0.0)
     peak[...] = jnp.full(peak.shape, -3e38, F32)
-
-    pl.semaphore_wait(barrier, n_dom + n_blk - 2)
-
-    core = lax.rem(me_b, 2)
-    x0 = lax.rem(me_b // 2, 4)
-    y0 = me_b // 8
-    x_right, x_left, x_far = lax.rem(x0 + 1, 4), lax.rem(x0 + 3, 4), lax.rem(x0 + 2, 4)
-    y1, other = 1 - y0, 1 - core
-
-    def block_id(y, x, c):
-        return (y * 4 + x) * 2 + c
-
-    sibling = block_id(y0, x0, other)
-    right, left = block_id(y0, x_right, core), block_id(y0, x_left, core)
-    across = block_id(y1, x0, core)
-    started = []
-
-    def send(part, block, device, half=None):
-        buffer = (kv, qg)[part]
-        ref = buffer.at[block] if half is None else buffer.at[block, half]
-        copy = pltpu.make_async_remote_copy(
-            src_ref=ref,
-            dst_ref=ref,
-            send_sem=ag_send.at[len(started)],
-            recv_sem=ag_recv.at[part, block, 0 if half is None else half],
-            device_id=(me_d, device),
-            device_id_type=MESH,
-        )
-        copy.start()
-        started.append(copy)
-
-    def arrived(part, block, half=None):
-        buffer = (kv, qg)[part]
-        ref = buffer.at[block] if half is None else buffer.at[block, half]
-        sem = ag_recv.at[part, block, 0 if half is None else half]
-        pltpu.make_async_copy(ref, ref, sem).wait()
-
-    def gather_own(part):
-        for device in (right, left, across, sibling):
-            send(part, me_b, device)
-
-    def gather_ring(part, y):
-        from_left, from_right = block_id(y, x_left, core), block_id(y, x_right, core)
-        arrived(part, from_left)
-        send(part, from_left, right, 0)
-        send(part, from_left, sibling)
-        arrived(part, from_right)
-        send(part, from_right, left, 1)
-        send(part, from_right, sibling)
-
-    def gather_across(part):
-        block = block_id(y1, x0, core)
-        arrived(part, block)
-        for device in (right, left, sibling):
-            send(part, block, device)
-
-    def gather_far(part, y):
-        block = block_id(y, x_far, core)
-        arrived(part, block, 0)
-        arrived(part, block, 1)
-        send(part, block, sibling)
-
-    gather_own(0)
-
-    def zigzag(step, size):
-        return jnp.where(lax.rem(step, 2) == 1, (step + 1) // 2, lax.rem(size - step // 2, size))
-
-    def at_offset(dz, dy):
-        z = lax.rem(me_d // 4 + dz + 16, 8)
-        y = lax.rem(lax.rem(me_d, 4) + dy + 8, 4)
-        return z * 4 + y
-
-    def legs(step, way):
-        along_z = step < 4
-        dz = jnp.where(along_z, 4, zigzag(step - 4, 8))
-        dy = jnp.where(along_z, step, 2)
-        first_z = jnp.where(along_z, 2 * way, dz)
-        first_y = jnp.where(dy == 2, way, dy)
-        return dz, dy, first_z, first_y
-
-    def push(source, target, send_sem, recv_sem, group):
-        pltpu.make_async_remote_copy(
-            src_ref=source,
-            dst_ref=target,
-            send_sem=send_sem,
-            recv_sem=recv_sem,
-            device_id=(group, me_b),
-            device_id_type=MESH,
-        ).start()
-
-    def exchange(source, relay, target, send_sem, mid_sem, recv_sem, phase):
-        way = 1 - 2 * phase
-
-        def indirect(step, carry):
-            dz, dy, first_z, first_y = legs(step, way)
-            push(
-                source.at[phase, at_offset(dz, dy)], relay.at[phase, step],
-                send_sem.at[phase], mid_sem.at[phase], at_offset(first_z, first_y),
-            )
-            return carry
-
-        def direct(step, carry):
-            group = at_offset(zigzag(step // 3, 8), zigzag(lax.rem(step, 3), 4))
-            push(source.at[phase, group], target.at[phase, me_d], send_sem.at[phase], recv_sem.at[phase], group)
-            return carry
-
-        lax.fori_loop(0, RELAYED, indirect, 0)
-        lax.fori_loop(1, 21, direct, 0)
-
-    def pass_on(relay, target, mid_sem, next_sem, recv_sem, phase):
-        way = 1 - 2 * phase
-        pltpu.make_async_copy(relay.at[phase], relay.at[phase], mid_sem.at[phase]).wait()
-
-        def one(step, carry):
-            dz, dy, first_z, first_y = legs(step, way)
-            push(
-                relay.at[phase, step], target.at[phase, at_offset(-first_z, -first_y)],
-                next_sem.at[phase], recv_sem.at[phase], at_offset(dz - first_z, dy - first_y),
-            )
-            return carry
-
-        lax.fori_loop(0, RELAYED, one, 0)
-
-    def exchanged(buffer, sem, phase):
-        ref = buffer.at[phase, pl.ds(0, n_dom - 1)]
-        pltpu.make_async_copy(ref, ref, sem.at[phase]).wait()
-
-    for phase in range(PHASES):
-        exchange(far_out, out_relay, far_in, far_send, far_mid, far_recv, phase)
 
     def score_chip(row, y, x):
         chip = y * 4 + x
@@ -355,12 +353,13 @@
     stat_cols[...] = jnp.zeros((BLOCK, 128), F32)
     for phase in range(PHASES):
         exchanged(far_in, far_recv, phase)
+        if phase == PHASES - 1:
+            send(1, me_b, across)
         for place in range(PER_PHASE):
             far_pair(phase, place)
         exchange(terms, back_relay, ret, ret_send, ret_mid, ret_recv, phase)
         if phase == 0:
             gather_ring(1, y0)
-            gather_across(1)
 
     stat_rows = stat_cols[...].T
     for block in range(n_blk):
@@ -401,10 +400,9 @@
     gather_far(1, y0)
     lax.fori_loop(0, PAIRS // 2, query_pair, 0)
     pass_on(*back_path, 0)
-    gather_ring(1, y1)
+    gather_across(1)
     lax.fori_loop(PAIRS // 2, PAIRS, query_pair, 0)
     pass_on(*back_path, 1)
-    gather_far(1, y1)
 
     def written(number, source, target):
         return pltpu.make_async_copy(source, target, out_sem.at[number])
@@ -415,21 +413,19 @@
 
     all_stats = stats_in.at[pl.ds(0, n_blk - 1)]
     pltpu.make_async_copy(all_stats, all_stats, stat_recv.at[0]).wait()
-    for y in (y0, y1):
-        for x in (x0, x_left, x_right, x_far):
-            arrived(1, block_id(y, x, other))
-
-    def key_pair(pair, carry):
+
+    def key_pair(row, y, pair, carry):
         lanes = lanes_of(pair)
         own_keys, own_values = kst[pair], vst[pair]
 
         def stat_row(start, row):
-            return jnp.concatenate([stats_in[start + n, pl.ds(row, 1), :] for n in range(4)], axis=1)
+            return jnp.concatenate([stats_in[y * row_blocks + start + n, pl.ds(row, 1), :] for n in range(4)], axis=1)
 
         sum_k = sum_v = jnp.zeros((256, 128), F32)
-        for start in range(0, n_blk, 4):
-            query_rows = qg[start : start + 4, 0, :, lanes].reshape(4 * BLOCK, 128)
-            grad_rows = qg[start : start + 4, 1, :, lanes].reshape(4 * BLOCK, 128)
+        for start in range(0, row_blocks, 4):
+            blocks = pl.ds(y * row_blocks + start, 4)
+            query_rows = qg[blocks, 0, :, lanes].reshape(4 * BLOCK, 128)
+            grad_rows = qg[blocks, 1, :, lanes].reshape(4 * BLOCK, 128)
             scores = dot_nt(own_keys, query_rows)
             moves = dot_nt(own_values, grad_rows)
             weights, slopes = [], []
@@ -440,11 +436,23 @@
                 slopes.append((chances * (moves[rows] - stat_row(start, HEADS + 2 * pair + head))).astype(BF16))
             sum_k += dot_nn(jnp.concatenate(slopes, axis=0), query_rows)
             sum_v += dot_nn(jnp.concatenate(weights, axis=0), grad_rows)
-        near_dk[pair] = jnp.where(low, sum_k[:BLOCK], sum_k[BLOCK:]) * 0.125
-        near_dv[pair] = jnp.where(low, sum_v[:BLOCK], sum_v[BLOCK:])
+        own_dk = jnp.where(low, sum_k[:BLOCK], sum_k[BLOCK:])
+        own_dv = jnp.where(low, sum_v[:BLOCK], sum_v[BLOCK:])
+        near_dk[pair] = own_dk if row == 0 else near_dk[pair] + own_dk
+        near_dv[pair] = own_dv if row == 0 else near_dv[pair] + own_dv
         return carry
 
-    lax.fori_loop(0, PAIRS, key_pair, 0)
+    def gathered(y):
+        for x in (x0, x_left, x_right, x_far):
+            arrived(1, block_id(y, x, other))
+
+    gathered(y0)
+    lax.fori_loop(0, PAIRS // 2, functools.partial(key_pair, 0, y0), 0)
+    gather_ring(1, y1)
+    lax.fori_loop(PAIRS // 2, PAIRS, functools.partial(key_pair, 0, y0), 0)
+    gather_far(1, y1)
+    gathered(y1)
+    lax.fori_loop(0, PAIRS, functools.partial(key_pair, 1, y1), 0)
 
     for phase in range(PHASES):
         exchanged(ret, ret_recv, phase)
@@ -454,7 +462,7 @@
             hits = picks[...]
             back_k = ret[phase, :, :, place * 256 : place * 256 + 128].reshape(far_rows, 128)
             back_v = ret[phase, :, :, place * 256 + 128 : place * 256 + 256].reshape(far_rows, 128)
-            dk_ref[:, cols] = (near_dk[pair] + dot_nn(hits, back_k)).astype(BF16)
+            dk_ref[:, cols] = (near_dk[pair] * 0.125 + dot_nn(hits, back_k)).astype(BF16)
             dv_ref[:, cols] = (near_dv[pair] + dot_nn(hits, back_v)).astype(BF16)
 
     dk_copy, dv_copy = written(2, dk_ref, dk_out), written(3, dv_ref, dv_out)
@@ -473,13 +481,17 @@
         copy.wait()
 
 
-def write_out(a, b, c, d, a_out, b_out, c_out, d_out, sems):
+def write_out(a, b, c, d, a_out, b_out, c_out, d_out, stage, sems):
     pairs = ((a, a_out), (b, b_out), (c, c_out), (d, d_out))
-    copies = [pltpu.make_async_copy(here, there, sems.at[n]) for n, (here, there) in enumerate(pairs)]
-    for copy in copies:
-        copy.start()
-    for copy in copies:
-        copy.wait()
+    reads = [pltpu.make_async_copy(pair[0], stage.at[n], sems.at[0, n]) for n, pair in enumerate(pairs)]
+    writes = [pltpu.make_async_copy(stage.at[n], pair[1], sems.at[1, n]) for n, pair in enumerate(pairs)]
+    for read in reads:
+        read.start()
+    for read, write in zip(reads, writes):
+        read.wait()
+        write.start()
+    for write in writes:
+        write.wait()
 
 
 def on_device(n_dom, n_blk, queries, keys, values, grad_out, tile_keys, tile_count, send_rows):
@@ -544,7 +556,7 @@
         out_shape=[jax.ShapeDtypeStruct((rows, width), BF16)] * 4,
         in_specs=[hbm] * 4,
         out_specs=[hbm] * 4,
-        scratch_shapes=[dma((4,))],
+        scratch_shapes=[pltpu.VMEM((4, rows, width), BF16), dma((2, 4))],
         compiler_params=pltpu.CompilerParams(vmem_limit_bytes=63 * 1024 * 1024),
     )(*held)
 

time: 106 us -> 97.3 us (0.918)
  the two profiles are of different devices: /device:TPU:49 before, /device:TPU:1 now
where the time goes in v3:
time: 97.3 us; the launch traced here: 95.8 us
  Pallas kernels  94.5 us (97%)
  between operations  1.29 us (1%)
    pallas_call x1, Pallas kernels, on_device(): pl.pallas_call(functools.partial(kernel, n_dom, n_blk), out_shape=[jax.Sh...  92.7 us

profile of v3, /device:TPU:1, one launch (start us, length us, event | category | flops | bytes accessed | tf_op | source)
XLA Modules:
  0.0 95.8 jit_solution(11305859420369646681)
XLA Ops:
  1.3 92.7 %shard_map.102 = (bf16[128,512]{1,0:T(8,128)(2,1)}, bf16[128,512]{1,0:T(8,128)(2,1)}, bf16[128,512]{1,0:T(8,128)(2,1)}, bf16[128,512]{1,0:T(8,128)(2,1)}) custom-call(bf16[128,512]{1,0:T(8,128)(2,1)} %q_in.1, bf16[128,512]{1,0:T(8,128)(2,1)} %k_in.1, bf16[128,512]{1,0:T(8,128)(2,1)} %v_in.1, bf16[128,512]{1,0:T(8,128)(2,1)} %g_in.1, s32[1,16]{1,0:T(1,128)} %order_in.1, ...), custom_call_target="tpu_custom_call" | custom-call | flops 2500000000 | bytes 2000000 | tf_op jit(solution)/shard_map/pallas_call | solution.py:513
  94.0 1.8 %shard_map.103 = (bf16[128,512]{1,0:T(8,128)(2,1)}, bf16[128,512]{1,0:T(8,128)(2,1)}, bf16[128,512]{1,0:T(8,128)(2,1)}, bf16[128,512]{1,0:T(8,128)(2,1)}) custom-call(bf16[128,512]{1,0:T(8,128)(2,1)} %get-tuple-element.8.a, bf16[128,512]{1,0:T(8,128)(2,1)} %get-tuple-element.9.b, bf16[128,512]{1,0:T(8,128)(2,1)} %get-tuple-element.10.c, ...), custom_call_target="tpu_custom_call" | custom-call | tf_op jit(solution)/shard_map/pallas_call | solution.py:554

commit v4 on v3

--- a/solution.py
+++ b/solution.py
@@ -142,8 +142,7 @@
 
     def gather_own(part):
         for device in (across, right, left, sibling):
-            if part == 0 or device is not across:
-                send(part, me_b, device)
+            send(part, me_b, device)
 
     def gather_ring(part, y):
         from_left, from_right = block_id(y, x_left, core), block_id(y, x_right, core)
@@ -353,13 +352,12 @@
     stat_cols[...] = jnp.zeros((BLOCK, 128), F32)
     for phase in range(PHASES):
         exchanged(far_in, far_recv, phase)
-        if phase == PHASES - 1:
-            send(1, me_b, across)
         for place in range(PER_PHASE):
             far_pair(phase, place)
         exchange(terms, back_relay, ret, ret_send, ret_mid, ret_recv, phase)
         if phase == 0:
             gather_ring(1, y0)
+            gather_across(1)
 
     stat_rows = stat_cols[...].T
     for block in range(n_blk):
@@ -398,11 +396,13 @@
         return carry
 
     gather_far(1, y0)
-    lax.fori_loop(0, PAIRS // 2, query_pair, 0)
+    lax.fori_loop(0, 2, query_pair, 0)
     pass_on(*back_path, 0)
-    gather_across(1)
-    lax.fori_loop(PAIRS // 2, PAIRS, query_pair, 0)
+    lax.fori_loop(2, 3, query_pair, 0)
     pass_on(*back_path, 1)
+    gather_ring(1, y1)
+    lax.fori_loop(3, PAIRS, query_pair, 0)
+    gather_far(1, y1)
 
     def written(number, source, target):
         return pltpu.make_async_copy(source, target, out_sem.at[number])
@@ -447,10 +447,7 @@
             arrived(1, block_id(y, x, other))
 
     gathered(y0)
-    lax.fori_loop(0, PAIRS // 2, functools.partial(key_pair, 0, y0), 0)
-    gather_ring(1, y1)
-    lax.fori_loop(PAIRS // 2, PAIRS, functools.partial(key_pair, 0, y0), 0)
-    gather_far(1, y1)
+    lax.fori_loop(0, PAIRS, functools.partial(key_pair, 0, y0), 0)
     gathered(y1)
     lax.fori_loop(0, PAIRS, functools.partial(key_pair, 1, y1), 0)
 

time: 97.3 us -> 94.2 us (0.968)
  the two profiles are of different devices: /device:TPU:1 before, /device:TPU:74 now
where the time goes in v4:
time: 94.2 us; the launch traced here: 94 us
  Pallas kernels  92.8 us (99%)
  between operations  1.29 us (1%)
    pallas_call x1, Pallas kernels, on_device(): pl.pallas_call(functools.partial(kernel, n_dom, n_blk), out_shape=[jax.Sh...  90.9 us

profile of v4, /device:TPU:74, one launch (start us, length us, event | category | flops | bytes accessed | tf_op | source)
XLA Modules:
  0.0 94.0 jit_solution(3392743957364957361)
XLA Ops:
  1.3 90.9 %shard_map.102 = (bf16[128,512]{1,0:T(8,128)(2,1)}, bf16[128,512]{1,0:T(8,128)(2,1)}, bf16[128,512]{1,0:T(8,128)(2,1)}, bf16[128,512]{1,0:T(8,128)(2,1)}) custom-call(bf16[128,512]{1,0:T(8,128)(2,1)} %q_in.1, bf16[128,512]{1,0:T(8,128)(2,1)} %k_in.1, bf16[128,512]{1,0:T(8,128)(2,1)} %v_in.1, bf16[128,512]{1,0:T(8,128)(2,1)} %g_in.1, s32[1,16]{1,0:T(1,128)} %order_in.1, ...), custom_call_target="tpu_custom_call" | custom-call | flops 2500000000 | bytes 2000000 | tf_op jit(solution)/shard_map/pallas_call | solution.py:510
  92.2 1.8 %shard_map.103 = (bf16[128,512]{1,0:T(8,128)(2,1)}, bf16[128,512]{1,0:T(8,128)(2,1)}, bf16[128,512]{1,0:T(8,128)(2,1)}, bf16[128,512]{1,0:T(8,128)(2,1)}) custom-call(bf16[128,512]{1,0:T(8,128)(2,1)} %get-tuple-element.8.a, bf16[128,512]{1,0:T(8,128)(2,1)} %get-tuple-element.9.b, bf16[128,512]{1,0:T(8,128)(2,1)} %get-tuple-element.10.c, ...), custom_call_target="tpu_custom_call" | custom-call | tf_op jit(solution)/shard_map/pallas_call | solution.py:551

commit v5 on v4

--- a/solution.py
+++ b/solution.py
@@ -53,19 +53,6 @@
     row_blocks = n_blk // 2
     row_keys = row_blocks * BLOCK
 
-    barrier = pltpu.get_barrier_semaphore()
-
-    def greet_dom(step, carry):
-        pl.semaphore_signal(barrier, inc=1, device_id=(lax.rem(me_d + step, n_dom), me_b), device_id_type=MESH)
-        return carry
-
-    def greet_blk(step, carry):
-        pl.semaphore_signal(barrier, inc=1, device_id=(me_d, lax.rem(me_b + step, n_blk)), device_id_type=MESH)
-        return carry
-
-    lax.fori_loop(1, n_blk, greet_blk, 0)
-    lax.fori_loop(1, n_dom, greet_dom, 0)
-
     loads = [
         pltpu.make_async_copy(source, target, in_sem.at[number])
         for number, (source, target) in enumerate(
@@ -81,29 +68,23 @@
     ]
     for load in loads:
         load.start()
-    for load in loads:
+
+    barrier = pltpu.get_barrier_semaphore()
+
+    def greet_dom(step, carry):
+        pl.semaphore_signal(barrier, inc=1, device_id=(lax.rem(me_d + step, n_dom), me_b), device_id_type=MESH)
+        return carry
+
+    def greet_blk(step, carry):
+        pl.semaphore_signal(barrier, inc=1, device_id=(me_d, lax.rem(me_b + step, n_blk)), device_id_type=MESH)
+        return carry
+
+    lax.fori_loop(1, n_blk, greet_blk, 0)
+    lax.fori_loop(1, n_dom, greet_dom, 0)
+
+    for load in loads[2:4]:
         load.wait()
     k_ref, v_ref, q_ref, g_ref = kv.at[me_b, 0], kv.at[me_b, 1], qg.at[me_b, 0], qg.at[me_b, 1]
-    group_of = lax.broadcasted_iota(jnp.int32, (n_dom, far_rows), 1) // SLOT
-    widen = jnp.where(group_of == lax.broadcasted_iota(jnp.int32, (n_dom, far_rows), 0), 1.0, 0.0).astype(BF16)
-    repeated = dot_nn(rows_ref[0].astype(F32).astype(BF16), widen)
-    slot_of = lax.rem(lax.broadcasted_iota(jnp.int32, (SLOT, far_rows), 1), SLOT)
-    slot = lax.broadcasted_iota(jnp.int32, (SLOT, far_rows), 0)
-    row_list = jnp.sum(jnp.where(slot_of == slot, repeated, 0.0), axis=0, keepdims=True)
-    node = lax.broadcasted_iota(jnp.int32, (BLOCK, far_rows), 0).astype(F32)
-    hits = jnp.where(row_list == node, 1.0, 0.0)
-    picks[...] = hits.astype(BF16)
-    spread = hits.T.astype(BF16)
-    low = lax.broadcasted_iota(jnp.int32, (BLOCK, 128), 1) < 64
-
-    for pair in range(PAIRS):
-        lanes = slice(pair * 128, pair * 128 + 128)
-        phase, place = divmod(pair, PER_PHASE)
-        k_own, v_own = k_ref[:, lanes], v_ref[:, lanes]
-        for own, first in ((k_own, place * 256), (v_own, place * 256 + 128)):
-            moved = dot_nn(spread, own).astype(BF16).reshape(n_dom, SLOT, 128)
-            far_out[phase, :, :, first : first + 128] = moved
-
     pl.semaphore_wait(barrier, n_dom + n_blk - 2)
 
     core = lax.rem(me_b, 2)
@@ -167,6 +148,28 @@
 
     gather_own(0)
 
+    for load in loads[:2] + loads[4:]:
+        load.wait()
+    group_of = lax.broadcasted_iota(jnp.int32, (n_dom, far_rows), 1) // SLOT
+    widen = jnp.where(group_of == lax.broadcasted_iota(jnp.int32, (n_dom, far_rows), 0), 1.0, 0.0).astype(BF16)
+    repeated = dot_nn(rows_ref[0].astype(F32).astype(BF16), widen)
+    slot_of = lax.rem(lax.broadcasted_iota(jnp.int32, (SLOT, far_rows), 1), SLOT)
+    slot = lax.broadcasted_iota(jnp.int32, (SLOT, far_rows), 0)
+    row_list = jnp.sum(jnp.where(slot_of == slot, repeated, 0.0), axis=0, keepdims=True)
+    node = lax.broadcasted_iota(jnp.int32, (BLOCK, far_rows), 0).astype(F32)
+    hits = jnp.where(row_list == node, 1.0, 0.0)
+    picks[...] = hits.astype(BF16)
+    spread = hits.T.astype(BF16)
+    low = lax.broadcasted_iota(jnp.int32, (BLOCK, 128), 1) < 64
+
+    for pair in range(PAIRS):
+        lanes = slice(pair * 128, pair * 128 + 128)
+        phase, place = divmod(pair, PER_PHASE)
+        k_own, v_own = k_ref[:, lanes], v_ref[:, lanes]
+        for own, first in ((k_own, place * 256), (v_own, place * 256 + 128)):
+            moved = dot_nn(spread, own).astype(BF16).reshape(n_dom, SLOT, 128)
+            far_out[phase, :, :, first : first + 128] = moved
+
     def zigzag(step, size):
         return jnp.where(lax.rem(step, 2) == 1, (step + 1) // 2, lax.rem(size - step // 2, size))
 
@@ -193,7 +196,7 @@
             device_id_type=MESH,
         ).start()
 
-    def exchange(source, relay, target, send_sem, mid_sem, recv_sem, phase):
+    def exchange(part, source, relay, target, send_sem, mid_sem, recv_sem, phase):
         way = 1 - 2 * phase
 
         def indirect(step, carry):
@@ -205,12 +208,15 @@
             return carry
 
         def direct(step, carry):
-            group = at_offset(zigzag(step // 3, 8), zigzag(lax.rem(step, 3), 4))
+            group = at_offset(zigzag(lax.rem(step, 7), 8), zigzag(step // 7, 4))
             push(source.at[phase, group], target.at[phase, me_d], send_sem.at[phase], recv_sem.at[phase], group)
             return carry
 
-        lax.fori_loop(0, RELAYED, indirect, 0)
-        lax.fori_loop(1, 21, direct, 0)
+        if "z" in part:
+            lax.fori_loop(1, 7, direct, 0)
+        if "y" in part:
+            lax.fori_loop(0, RELAYED, indirect, 0)
+            lax.fori_loop(7, 21, direct, 0)
 
     def pass_on(relay, target, mid_sem, next_sem, recv_sem, phase):
         way = 1 - 2 * phase
@@ -230,8 +236,9 @@
         ref = buffer.at[phase, pl.ds(0, n_dom - 1)]
         pltpu.make_async_copy(ref, ref, sem.at[phase]).wait()
 
-    for phase in range(PHASES):
-        exchange(far_out, out_relay, far_in, far_send, far_mid, far_recv, phase)
+    for part in ("z", "y"):
+        for phase in range(PHASES):
+            exchange(part, far_out, out_relay, far_in, far_send, far_mid, far_recv, phase)
 
     for pair in range(PAIRS):
         lanes = slice(pair * 128, pair * 128 + 128)
@@ -354,7 +361,7 @@
         exchanged(far_in, far_recv, phase)
         for place in range(PER_PHASE):
             far_pair(phase, place)
-        exchange(terms, back_relay, ret, ret_send, ret_mid, ret_recv, phase)
+        exchange("zy", terms, back_relay, ret, ret_send, ret_mid, ret_recv, phase)
         if phase == 0:
             gather_ring(1, y0)
             gather_across(1)

time: 94.2 us -> 96.3 us (1.022)
  the two profiles are of different devices: /device:TPU:74 before, /device:TPU:1 now
where the time goes in v5:
time: 96.3 us; the launch traced here: 95 us
  Pallas kernels  93.7 us (97%)
  between operations  1.29 us (1%)
    pallas_call x1, Pallas kernels, on_device(): pl.pallas_call(functools.partial(kernel, n_dom, n_blk), out_shape=[jax.Sh...  91.9 us

profile of v5, /device:TPU:1, one launch (start us, length us, event | category | flops | bytes accessed | tf_op | source)
XLA Modules:
  0.0 95.0 jit_solution(11092243828721695799)
XLA Ops:
  1.3 91.9 %shard_map.102 = (bf16[128,512]{1,0:T(8,128)(2,1)}, bf16[128,512]{1,0:T(8,128)(2,1)}, bf16[128,512]{1,0:T(8,128)(2,1)}, bf16[128,512]{1,0:T(8,128)(2,1)}) custom-call(bf16[128,512]{1,0:T(8,128)(2,1)} %q_in.1, bf16[128,512]{1,0:T(8,128)(2,1)} %k_in.1, bf16[128,512]{1,0:T(8,128)(2,1)} %v_in.1, bf16[128,512]{1,0:T(8,128)(2,1)} %g_in.1, s32[1,16]{1,0:T(1,128)} %order_in.1, ...), custom_call_target="tpu_custom_call" | custom-call | flops 2500000000 | bytes 2000000 | tf_op jit(solution)/shard_map/pallas_call | solution.py:517
  93.2 1.8 %shard_map.103 = (bf16[128,512]{1,0:T(8,128)(2,1)}, bf16[128,512]{1,0:T(8,128)(2,1)}, bf16[128,512]{1,0:T(8,128)(2,1)}, bf16[128,512]{1,0:T(8,128)(2,1)}) custom-call(bf16[128,512]{1,0:T(8,128)(2,1)} %get-tuple-element.8.a, bf16[128,512]{1,0:T(8,128)(2,1)} %get-tuple-element.9.b, bf16[128,512]{1,0:T(8,128)(2,1)} %get-tuple-element.10.c, ...), custom_call_target="tpu_custom_call" | custom-call | tf_op jit(solution)/shard_map/pallas_call | solution.py:558

commit v6 on v5

--- a/solution.py
+++ b/solution.py
@@ -42,7 +42,7 @@
     att_out, dq_out, dk_out, dv_out,
     kv, qg, far_out, far_in, terms, ret, out_relay, back_relay, stats_out, stats_in,
     order_ref, rows_ref, qst, gst, kst, vst, picks, bias, far_bias,
-    s_near, p_near, peak, m_near, l_near, a_near, factor, delta_ref, far_dq, near_dk, near_dv, stat_cols,
+    s_near, p_near, d_near, peak, m_near, l_near, a_near, factor, delta_ref, far_slopes, near_dk, near_dv, stat_cols,
     in_sem, ag_send, ag_recv, far_send, far_recv, far_mid, far_next, ret_send, ret_recv, ret_mid, ret_next,
     stat_send, stat_recv, att_ref, dq_ref, dk_ref, dv_ref, out_sem,
 ):
@@ -289,6 +289,14 @@
 
         lax.fori_loop(0, PAIRS, one, 0)
 
+    def move(row, y):
+        def one(pair, carry):
+            value_rows = kv[pl.ds(y * row_blocks, row_blocks), 1, :, lanes_of(pair)].reshape(row_keys, 128)
+            d_near[row, pair] = dot_nt(gst[pair], value_rows)
+            return carry
+
+        lax.fori_loop(0, PAIRS, one, 0)
+
     out_path = (out_relay, far_in, far_mid, far_next, far_recv)
     back_path = (back_relay, ret, ret_mid, ret_next, ret_recv)
 
@@ -306,10 +314,12 @@
     pass_on(*out_path, 1)
     gather_far(0, y1)
     gather_own(1)
+    move(0, y0)
     score_sibling(1, x_left)
     score_sibling(1, x_right)
     score_sibling(1, x_far)
     weigh(1, y1)
+    move(1, y1)
 
     column = lax.broadcasted_iota(jnp.int32, (BLOCK, 128), 1)
 
@@ -345,7 +355,7 @@
         slopes = (chances * (moves - delta)).astype(BF16)
         terms[phase, :, :, k_lanes] = dot_tn(slopes, queries).astype(BF16).reshape(n_dom, SLOT, 128)
         terms[phase, :, :, v_lanes] = dot_tn(weights, cotangent).astype(BF16).reshape(n_dom, SLOT, 128)
-        far_dq[pair] = dot_nn(slopes, key_rows)
+        far_slopes[pair] = slopes
         factor[0, pair] = scale0
         factor[1, pair] = scale1
         delta_ref[pair] = delta
@@ -389,14 +399,14 @@
 
     def query_pair(pair, carry):
         lanes = lanes_of(pair)
-        cotangent, delta = gst[pair], delta_ref[pair]
-        both = far_dq[pair]
+        delta = delta_ref[pair]
+        phase = pair // PER_PHASE
+        first = pl.multiple_of(lax.rem(pair, PER_PHASE) * 256, 256)
+        both = dot_nn(far_slopes[pair], far_in[phase, :, :, pl.ds(first, 128)].reshape(far_rows, 128))
         for row, y in enumerate((y0, y1)):
             blocks = pl.ds(y * row_blocks, row_blocks)
             key_rows = kv[blocks, 0, :, lanes].reshape(row_keys, 128)
-            value_rows = kv[blocks, 1, :, lanes].reshape(row_keys, 128)
-            moves = dot_nt(cotangent, value_rows)
-            slopes = (p_near[row, pair].astype(F32) * (moves - delta)).astype(BF16)
+            slopes = (p_near[row, pair].astype(F32) * (d_near[row, pair] - delta)).astype(BF16)
             both += dot_nn(slopes, key_rows) * factor[row, pair]
         both *= 0.125
         dq_ref[:, lanes] = jnp.where(low, both[:BLOCK], both[BLOCK:]).astype(BF16)
@@ -537,11 +547,12 @@
             pltpu.VMEM((1, far_rows), F32),
             pltpu.VMEM((2, PAIRS, 256, row_keys), F32),
             pltpu.VMEM((2, PAIRS, 256, row_keys), BF16),
+            pltpu.VMEM((2, PAIRS, 256, row_keys), F32),
             wide_rows,
             thin_rows, thin_rows,
             wide_rows,
             thin_rows, thin,
-            wide,
+            pltpu.VMEM((PAIRS, 256, far_rows), BF16),
             own, own,
             pltpu.VMEM((BLOCK, 128), F32),
             dma((6,)), dma((34,)), dma((2, n_blk, 2)),

time: 96.3 us -> 98.7 us (1.025); the launches traced: 95 us -> 98.5 us
  Pallas kernels: 93.7 us -> 97.2 us
    pallas_call x1, Pallas kernels: 91.9 us -> 95.4 us  [on_device(): pl.pallas_call(functools.partial(kernel, n_dom, n_blk), out_shape=[jax.Sh...]
where the time goes in v6:
time: 98.7 us; the launch traced here: 98.5 us
  Pallas kernels  97.2 us (98%)
  between operations  1.29 us (1%)
    pallas_call x1, Pallas kernels, on_device(): pl.pallas_call(functools.partial(kernel, n_dom, n_blk), out_shape=[jax.Sh...  95.4 us

profile of v6, /device:TPU:1, one launch (start us, length us, event | category | flops | bytes accessed | tf_op | source)
XLA Modules:
  0.0 98.5 jit_solution(16351687378304820447)
XLA Ops:
  1.3 95.4 %shard_map.102 = (bf16[128,512]{1,0:T(8,128)(2,1)}, bf16[128,512]{1,0:T(8,128)(2,1)}, bf16[128,512]{1,0:T(8,128)(2,1)}, bf16[128,512]{1,0:T(8,128)(2,1)}) custom-call(bf16[128,512]{1,0:T(8,128)(2,1)} %q_in.1, bf16[128,512]{1,0:T(8,128)(2,1)} %k_in.1, bf16[128,512]{1,0:T(8,128)(2,1)} %v_in.1, bf16[128,512]{1,0:T(8,128)(2,1)} %g_in.1, s32[1,16]{1,0:T(1,128)} %order_in.1, ...), custom_call_target="tpu_custom_call" | custom-call | flops 2500000000 | bytes 2000000 | tf_op jit(solution)/shard_map/pallas_call | solution.py:527
  96.7 1.8 %shard_map.103 = (bf16[128,512]{1,0:T(8,128)(2,1)}, bf16[128,512]{1,0:T(8,128)(2,1)}, bf16[128,512]{1,0:T(8,128)(2,1)}, bf16[128,512]{1,0:T(8,128)(2,1)}) custom-call(bf16[128,512]{1,0:T(8,128)(2,1)} %get-tuple-element.8.a, bf16[128,512]{1,0:T(8,128)(2,1)} %get-tuple-element.9.b, bf16[128,512]{1,0:T(8,128)(2,1)} %get-tuple-element.10.c, ...), custom_call_target="tpu_custom_call" | custom-call | tf_op jit(solution)/shard_map/pallas_call | solution.py:569

commit v7 on v4

--- a/solution.py
+++ b/solution.py
@@ -14,6 +14,7 @@
 BLOCK = 128
 SLOT = 16
 RELAYED = 11
+STRIP = 16
 HIDDEN = -1e30
 MESH = pl.DeviceIdType.MESH
 F32 = jnp.float32
@@ -42,7 +43,7 @@
     att_out, dq_out, dk_out, dv_out,
     kv, qg, far_out, far_in, terms, ret, out_relay, back_relay, stats_out, stats_in,
     order_ref, rows_ref, qst, gst, kst, vst, picks, bias, far_bias,
-    s_near, p_near, peak, m_near, l_near, a_near, factor, delta_ref, far_dq, near_dk, near_dv, stat_cols,
+    s_near, p_near, wide_a, wide_b, thin_a, thin_b, peak, m_near, l_near, a_near, factor, delta_ref, far_dq, near_dk, near_dv, stat_cols,
     in_sem, ag_send, ag_recv, far_send, far_recv, far_mid, far_next, ret_send, ret_recv, ret_mid, ret_next,
     stat_send, stat_recv, att_ref, dq_ref, dk_ref, dv_ref, out_sem,
 ):
@@ -271,13 +272,14 @@
     def weigh(row, y):
         def one(pair, carry):
             top = jnp.max(peak[row, pair], axis=1, keepdims=True)
-            exps = jnp.exp(s_near[row, pair] - top)
-            narrow = exps.astype(BF16)
-            p_near[row, pair] = narrow
+            m_near[row, pair] = top
+            for first in range(0, 256, STRIP):
+                strip = slice(first, first + STRIP)
+                exps = jnp.exp(s_near[row, pair, strip, :] - top[strip])
+                p_near[row, pair, strip, :] = exps.astype(BF16)
+                l_near[row, pair, strip, :] = jnp.sum(exps, axis=1, keepdims=True)
             value_rows = kv[pl.ds(y * row_blocks, row_blocks), 1, :, lanes_of(pair)].reshape(row_keys, 128)
-            m_near[row, pair] = top
-            l_near[row, pair] = jnp.sum(exps, axis=1, keepdims=True)
-            a_near[row, pair] = dot_nn(narrow, value_rows)
+            a_near[row, pair] = dot_nn(p_near[row, pair], value_rows)
             return carry
 
         lax.fori_loop(0, PAIRS, one, 0)
@@ -313,12 +315,19 @@
         key_rows = far_in[phase, :, :, k_lanes].reshape(far_rows, 128)
         value_rows = far_in[phase, :, :, v_lanes].reshape(far_rows, 128)
         queries, cotangent = qst[pair], gst[pair]
-        scores = dot_nt(queries, key_rows) + far_bias[...]
-        moves = dot_nt(cotangent, value_rows)
-        top = jnp.max(scores, axis=1, keepdims=True)
-        exps = jnp.exp(scores - top)
-        total = jnp.sum(exps, axis=1, keepdims=True)
-        far_att = dot_nn(exps.astype(BF16), value_rows)
+        wide_a[place, :, :far_rows] = dot_nt(queries, key_rows) + far_bias[...]
+        wide_b[place, :, :far_rows] = dot_nt(cotangent, value_rows)
+        strips = [slice(first, first + STRIP) for first in range(0, 256, STRIP)]
+        tops, totals = [], []
+        for strip in strips:
+            scores = wide_a[place, strip, :far_rows]
+            tops.append(jnp.max(scores, axis=1, keepdims=True))
+            exps = jnp.exp(scores - tops[-1])
+            totals.append(jnp.sum(exps, axis=1, keepdims=True))
+            wide_a[place, strip, :far_rows] = exps
+            thin_a[place, strip, :far_rows] = exps.astype(BF16)
+        top, total = jnp.concatenate(tops, axis=0), jnp.concatenate(totals, axis=0)
+        far_att = dot_nn(thin_a[place, :, :far_rows], value_rows)
         top0, top1 = m_near[0, pair], m_near[1, pair]
         highest = jnp.maximum(top, jnp.maximum(top0, top1))
         scale0, scale1 = jnp.exp(top0 - highest), jnp.exp(top1 - highest)
@@ -333,9 +342,11 @@
         delta1 = jnp.sum(jnp.where(low, 0.0, product), axis=1, keepdims=True)
         delta = jnp.concatenate([delta0, delta1], axis=0)
         log_total = highest + jnp.log(whole)
-        chances = exps * far_scale
-        weights = chances.astype(BF16)
-        slopes = (chances * (moves - delta)).astype(BF16)
+        for strip in strips:
+            chances = wide_a[place, strip, :far_rows] * far_scale[strip]
+            thin_a[place, strip, :far_rows] = chances.astype(BF16)
+            thin_b[place, strip, :far_rows] = (chances * (wide_b[place, strip, :far_rows] - delta[strip])).astype(BF16)
+        weights, slopes = thin_a[place, :, :far_rows], thin_b[place, :, :far_rows]
         terms[phase, :, :, k_lanes] = dot_tn(slopes, queries).astype(BF16).reshape(n_dom, SLOT, 128)
         terms[phase, :, :, v_lanes] = dot_tn(weights, cotangent).astype(BF16).reshape(n_dom, SLOT, 128)
         far_dq[pair] = dot_nn(slopes, key_rows)
@@ -388,9 +399,12 @@
             blocks = pl.ds(y * row_blocks, row_blocks)
             key_rows = kv[blocks, 0, :, lanes].reshape(row_keys, 128)
             value_rows = kv[blocks, 1, :, lanes].reshape(row_keys, 128)
-            moves = dot_nt(cotangent, value_rows)
-            slopes = (p_near[row, pair].astype(F32) * (moves - delta)).astype(BF16)
-            both += dot_nn(slopes, key_rows) * factor[row, pair]
+            wide_a[row] = dot_nt(cotangent, value_rows)
+            for first in range(0, 256, STRIP):
+                strip = slice(first, first + STRIP)
+                slopes = p_near[row, pair, strip, :].astype(F32) * (wide_a[row, strip, :] - delta[strip])
+                thin_a[row, strip, :] = slopes.astype(BF16)
+            both += dot_nn(thin_a[row], key_rows) * factor[row, pair]
         both *= 0.125
         dq_ref[:, lanes] = jnp.where(low, both[:BLOCK], both[BLOCK:]).astype(BF16)
         return carry
@@ -418,24 +432,25 @@
         lanes = lanes_of(pair)
         own_keys, own_values = kst[pair], vst[pair]
 
-        def stat_row(start, row):
-            return jnp.concatenate([stats_in[y * row_blocks + start + n, pl.ds(row, 1), :] for n in range(4)], axis=1)
-
-        sum_k = sum_v = jnp.zeros((256, 128), F32)
-        for start in range(0, row_blocks, 4):
-            blocks = pl.ds(y * row_blocks + start, 4)
-            query_rows = qg[blocks, 0, :, lanes].reshape(4 * BLOCK, 128)
-            grad_rows = qg[blocks, 1, :, lanes].reshape(4 * BLOCK, 128)
-            scores = dot_nt(own_keys, query_rows)
-            moves = dot_nt(own_values, grad_rows)
-            weights, slopes = [], []
-            for head in range(2):
-                rows = slice(head * BLOCK, head * BLOCK + BLOCK)
-                chances = jnp.exp(scores[rows] - stat_row(start, 2 * pair + head))
-                weights.append(chances.astype(BF16))
-                slopes.append((chances * (moves[rows] - stat_row(start, HEADS + 2 * pair + head))).astype(BF16))
-            sum_k += dot_nn(jnp.concatenate(slopes, axis=0), query_rows)
-            sum_v += dot_nn(jnp.concatenate(weights, axis=0), grad_rows)
+        def stat_row(line):
+            return jnp.concatenate(
+                [stats_in[y * row_blocks + n, pl.ds(line, 1), :] for n in range(row_blocks)], axis=1
+            )
+
+        blocks = pl.ds(y * row_blocks, row_blocks)
+        query_rows = qg[blocks, 0, :, lanes].reshape(row_keys, 128)
+        grad_rows = qg[blocks, 1, :, lanes].reshape(row_keys, 128)
+        wide_a[row] = dot_nt(own_keys, query_rows)
+        wide_b[row] = dot_nt(own_values, grad_rows)
+        for head in range(2):
+            log_row, delta_row = stat_row(2 * pair + head), stat_row(HEADS + 2 * pair + head)
+            for first in range(head * BLOCK, head * BLOCK + BLOCK, STRIP):
+                strip = slice(first, first + STRIP)
+                chances = jnp.exp(wide_a[row, strip, :] - log_row)
+                thin_a[row, strip, :] = chances.astype(BF16)
+                thin_b[row, strip, :] = (chances * (wide_b[row, strip, :] - delta_row)).astype(BF16)
+        sum_k = dot_nn(thin_b[row], query_rows)
+        sum_v = dot_nn(thin_a[row], grad_rows)
         own_dk = jnp.where(low, sum_k[:BLOCK], sum_k[BLOCK:])
         own_dv = jnp.where(low, sum_v[:BLOCK], sum_v[BLOCK:])
         near_dk[pair] = own_dk if row == 0 else near_dk[pair] + own_dk
@@ -530,6 +545,10 @@
             pltpu.VMEM((1, far_rows), F32),
             pltpu.VMEM((2, PAIRS, 256, row_keys), F32),
             pltpu.VMEM((2, PAIRS, 256, row_keys), BF16),
+            pltpu.VMEM((2, 256, row_keys), F32),
+            pltpu.VMEM((2, 256, row_keys), F32),
+            pltpu.VMEM((2, 256, row_keys), BF16),
+            pltpu.VMEM((2, 256, row_keys), BF16),
             wide_rows,
             thin_rows, thin_rows,
             wide_rows,

time: 94.2 us -> 93.5 us (level)
  no operation moved by 1% of the time
where the time goes in v7:
time: 93.5 us; the launch traced here: 93.3 us
  Pallas kernels  92.1 us (99%)
  between operations  1.29 us (1%)
    pallas_call x1, Pallas kernels, on_device(): pl.pallas_call(functools.partial(kernel, n_dom, n_blk), out_shape=[jax.Sh...  90.2 us

profile of v7, /device:TPU:74, one launch (start us, length us, event | category | flops | bytes accessed | tf_op | source)
XLA Modules:
  0.0 93.3 jit_solution(1703044532383882254)
XLA Ops:
  1.3 90.2 %shard_map.102 = (bf16[128,512]{1,0:T(8,128)(2,1)}, bf16[128,512]{1,0:T(8,128)(2,1)}, bf16[128,512]{1,0:T(8,128)(2,1)}, bf16[128,512]{1,0:T(8,128)(2,1)}) custom-call(bf16[128,512]{1,0:T(8,128)(2,1)} %q_in.1, bf16[128,512]{1,0:T(8,128)(2,1)} %k_in.1, bf16[128,512]{1,0:T(8,128)(2,1)} %v_in.1, bf16[128,512]{1,0:T(8,128)(2,1)} %g_in.1, s32[1,16]{1,0:T(1,128)} %order_in.1, ...), custom_call_target="tpu_custom_call" | custom-call | flops 2500000000 | bytes 2000000 | tf_op jit(solution)/shard_map/pallas_call | solution.py:525
  91.5 1.8 %shard_map.103 = (bf16[128,512]{1,0:T(8,128)(2,1)}, bf16[128,512]{1,0:T(8,128)(2,1)}, bf16[128,512]{1,0:T(8,128)(2,1)}, bf16[128,512]{1,0:T(8,128)(2,1)}) custom-call(bf16[128,512]{1,0:T(8,128)(2,1)} %get-tuple-element.8.a, bf16[128,512]{1,0:T(8,128)(2,1)} %get-tuple-element.9.b, bf16[128,512]{1,0:T(8,128)(2,1)} %get-tuple-element.10.c, ...), custom_call_target="tpu_custom_call" | custom-call | tf_op jit(solution)/shard_map/pallas_call | solution.py:570

commit v8 on v7

--- a/solution.py
+++ b/solution.py
@@ -13,7 +13,6 @@
 PER_PHASE = PAIRS // PHASES
 BLOCK = 128
 SLOT = 16
-RELAYED = 11
 STRIP = 16
 HIDDEN = -1e30
 MESH = pl.DeviceIdType.MESH
@@ -41,10 +40,10 @@
     n_dom, n_blk,
     q_in, k_in, v_in, g_in, order_in, count_ref, rows_in,
     att_out, dq_out, dk_out, dv_out,
-    kv, qg, far_out, far_in, terms, ret, out_relay, back_relay, stats_out, stats_in,
+    kv, qg, far_out, far_in, terms, ret, stats_out, stats_in,
     order_ref, rows_ref, qst, gst, kst, vst, picks, bias, far_bias,
     s_near, p_near, wide_a, wide_b, thin_a, thin_b, peak, m_near, l_near, a_near, factor, delta_ref, far_dq, near_dk, near_dv, stat_cols,
-    in_sem, ag_send, ag_recv, far_send, far_recv, far_mid, far_next, ret_send, ret_recv, ret_mid, ret_next,
+    in_sem, ag_send, ag_recv, far_send, far_recv, ret_send, ret_recv,
     stat_send, stat_recv, att_ref, dq_ref, dk_ref, dv_ref, out_sem,
 ):
     me_d = lax.axis_index("dom")
@@ -176,14 +175,6 @@
         y = lax.rem(lax.rem(me_d, 4) + dy + 8, 4)
         return z * 4 + y
 
-    def legs(step, way):
-        along_z = step < 4
-        dz = jnp.where(along_z, 4, zigzag(step - 4, 8))
-        dy = jnp.where(along_z, step, 2)
-        first_z = jnp.where(along_z, 2 * way, dz)
-        first_y = jnp.where(dy == 2, way, dy)
-        return dz, dy, first_z, first_y
-
     def push(source, target, send_sem, recv_sem, group):
         pltpu.make_async_remote_copy(
             src_ref=source,
@@ -194,45 +185,20 @@
             device_id_type=MESH,
         ).start()
 
-    def exchange(source, relay, target, send_sem, mid_sem, recv_sem, phase):
-        way = 1 - 2 * phase
-
-        def indirect(step, carry):
-            dz, dy, first_z, first_y = legs(step, way)
-            push(
-                source.at[phase, at_offset(dz, dy)], relay.at[phase, step],
-                send_sem.at[phase], mid_sem.at[phase], at_offset(first_z, first_y),
-            )
-            return carry
-
+    def exchange(source, target, send_sem, recv_sem, phase):
         def direct(step, carry):
-            group = at_offset(zigzag(step // 3, 8), zigzag(lax.rem(step, 3), 4))
+            group = at_offset(zigzag(lax.rem(step, 8), 8), zigzag(step // 8, 4))
             push(source.at[phase, group], target.at[phase, me_d], send_sem.at[phase], recv_sem.at[phase], group)
             return carry
 
-        lax.fori_loop(0, RELAYED, indirect, 0)
-        lax.fori_loop(1, 21, direct, 0)
-
-    def pass_on(relay, target, mid_sem, next_sem, recv_sem, phase):
-        way = 1 - 2 * phase
-        pltpu.make_async_copy(relay.at[phase], relay.at[phase], mid_sem.at[phase]).wait()
-
-        def one(step, carry):
-            dz, dy, first_z, first_y = legs(step, way)
-            push(
-                relay.at[phase, step], target.at[phase, at_offset(-first_z, -first_y)],
-                next_sem.at[phase], recv_sem.at[phase], at_offset(dz - first_z, dy - first_y),
-            )
-            return carry
-
-        lax.fori_loop(0, RELAYED, one, 0)
+        lax.fori_loop(1, n_dom, direct, 0)
 
     def exchanged(buffer, sem, phase):
         ref = buffer.at[phase, pl.ds(0, n_dom - 1)]
         pltpu.make_async_copy(ref, ref, sem.at[phase]).wait()
 
     for phase in range(PHASES):
-        exchange(far_out, out_relay, far_in, far_send, far_mid, far_recv, phase)
+        exchange(far_out, far_in, far_send, far_recv, phase)
 
     for pair in range(PAIRS):
         lanes = slice(pair * 128, pair * 128 + 128)
@@ -284,21 +250,16 @@
 
         lax.fori_loop(0, PAIRS, one, 0)
 
-    out_path = (out_relay, far_in, far_mid, far_next, far_recv)
-    back_path = (back_relay, ret, ret_mid, ret_next, ret_recv)
-
     score_sibling(0, x0)
     gather_ring(0, y0)
     gather_across(0)
     score_sibling(0, x_left)
     score_sibling(0, x_right)
     gather_far(0, y0)
-    pass_on(*out_path, 0)
     score_sibling(0, x_far)
     score_sibling(1, x0)
     gather_ring(0, y1)
     weigh(0, y0)
-    pass_on(*out_path, 1)
     gather_far(0, y1)
     gather_own(1)
     score_sibling(1, x_left)
@@ -365,7 +326,7 @@
         exchanged(far_in, far_recv, phase)
         for place in range(PER_PHASE):
             far_pair(phase, place)
-        exchange(terms, back_relay, ret, ret_send, ret_mid, ret_recv, phase)
+        exchange(terms, ret, ret_send, ret_recv, phase)
         if phase == 0:
             gather_ring(1, y0)
             gather_across(1)
@@ -410,10 +371,7 @@
         return carry
 
     gather_far(1, y0)
-    lax.fori_loop(0, 2, query_pair, 0)
-    pass_on(*back_path, 0)
-    lax.fori_loop(2, 3, query_pair, 0)
-    pass_on(*back_path, 1)
+    lax.fori_loop(0, 3, query_pair, 0)
     gather_ring(1, y1)
     lax.fori_loop(3, PAIRS, query_pair, 0)
     gather_far(1, y1)
@@ -485,8 +443,6 @@
     for phase in range(PHASES):
         exchanged(far_out, far_send, phase)
         exchanged(terms, ret_send, phase)
-        pltpu.make_async_copy(out_relay.at[phase], out_relay.at[phase], far_next.at[phase]).wait()
-        pltpu.make_async_copy(back_relay.at[phase], back_relay.at[phase], ret_next.at[phase]).wait()
     sent_stats = stats_out.at[pl.ds(0, n_blk - 1)]
     pltpu.make_async_copy(sent_stats, sent_stats, stat_send.at[0]).wait()
     for copy in (att_copy, dq_copy, dk_copy, dv_copy):
@@ -514,7 +470,6 @@
     smem = pl.BlockSpec(memory_space=pltpu.SMEM)
     far_shape = (PHASES, n_dom, SLOT, PER_PHASE * 256)
     stack = pltpu.VMEM((PAIRS, 256, 128), BF16)
-    relay = pltpu.VMEM((PHASES, RELAYED, SLOT, PER_PHASE * 256), BF16)
     wide = pltpu.VMEM((PAIRS, 256, 128), F32)
     wide_rows = pltpu.VMEM((2, PAIRS, 256, 128), F32)
     thin = pltpu.VMEM((PAIRS, 256, 1), F32)
@@ -534,7 +489,6 @@
             pltpu.VMEM(far_shape, BF16),
             pltpu.VMEM(far_shape, BF16),
             pltpu.VMEM(far_shape, BF16),
-            relay, relay,
             pltpu.VMEM((n_blk, 2 * HEADS, BLOCK), F32),
             pltpu.VMEM((n_blk, 2 * HEADS, BLOCK), F32),
             pltpu.SMEM((1, n_blk), jnp.int32),
@@ -558,7 +512,6 @@
             pltpu.VMEM((BLOCK, 128), F32),
             dma((6,)), dma((34,)), dma((2, n_blk, 2)),
             dma((PHASES,)), dma((PHASES,)), dma((PHASES,)), dma((PHASES,)),
-            dma((PHASES,)), dma((PHASES,)), dma((PHASES,)), dma((PHASES,)),
             dma((1,)), dma((1,)),
             whole, whole, whole, whole, dma((4,)),
         ],

time: 93.5 us -> 88.3 us (0.944)
  the two profiles are of different devices: /device:TPU:74 before, /device:TPU:1 now
where the time goes in v8:
time: 88.3 us; the launch traced here: 88.1 us
  Pallas kernels  86.8 us (98%)
  between operations  1.29 us (1%)
    pallas_call x1, Pallas kernels, on_device(): pl.pallas_call(functools.partial(kernel, n_dom, n_blk), out_shape=[jax.Sh...  85 us
    pallas_call x1, Pallas kernels, on_device(): pl.pallas_call(write_out, out_shape=[jax.ShapeDtypeStruct((rows, width),...  1.82 us

profile of v8, /device:TPU:1, one launch (start us, length us, event | category | flops | bytes accessed | tf_op | source)
XLA Modules:
  0.0 88.1 jit_solution(1874615322755648814)
XLA Ops:
  1.3 85.0 %shard_map.102 = (bf16[128,512]{1,0:T(8,128)(2,1)}, bf16[128,512]{1,0:T(8,128)(2,1)}, bf16[128,512]{1,0:T(8,128)(2,1)}, bf16[128,512]{1,0:T(8,128)(2,1)}) custom-call(bf16[128,512]{1,0:T(8,128)(2,1)} %q_in.1, bf16[128,512]{1,0:T(8,128)(2,1)} %k_in.1, bf16[128,512]{1,0:T(8,128)(2,1)} %v_in.1, bf16[128,512]{1,0:T(8,128)(2,1)} %g_in.1, s32[1,16]{1,0:T(1,128)} %order_in.1, ...), custom_call_target="tpu_custom_call" | custom-call | flops 2500000000 | bytes 2000000 | tf_op jit(solution)/shard_map/pallas_call | solution.py:480
  86.3 1.8 %shard_map.103 = (bf16[128,512]{1,0:T(8,128)(2,1)}, bf16[128,512]{1,0:T(8,128)(2,1)}, bf16[128,512]{1,0:T(8,128)(2,1)}, bf16[128,512]{1,0:T(8,128)(2,1)}) custom-call(bf16[128,512]{1,0:T(8,128)(2,1)} %get-tuple-element.8.a, bf16[128,512]{1,0:T(8,128)(2,1)} %get-tuple-element.9.b, bf16[128,512]{1,0:T(8,128)(2,1)} %get-tuple-element.10.c, ...), custom_call_target="tpu_custom_call" | custom-call | tf_op jit(solution)/shard_map/pallas_call | solution.py:523
